TPU v7x, 32 devices: a whole 2x2x4 slice. The times are simulated.
32 devices in a mesh: groups: 2 (over y), dap: 4 (over z), chan: 2 (over x), sub: 2 (over core).
Axes of the slice: x: 2, y: 2, z: 4, core: 2. Of those that a mesh axis runs over, the one named last changes fastest.
Arguments:
- pair_input: bfloat16 [768, 384, 128], P(('groups', 'dap'), ('chan', 'sub')), parts along dimension 0, may hold values from -6 to 6
- first_gain: float32 [128], replicated, may hold values from 0.25 to 1.75
- first_project: bfloat16 [128, 512], replicated, may hold values from -0.5 to 0.5
- first_gate: bfloat16 [128, 128], replicated, may hold values from -0.5 to 0.5
- first_norm: float32 [128], replicated, may hold values from 0.25 to 1.75
- first_final: bfloat16 [128, 128], replicated, may hold values from -0.5 to 0.5
- second_gain: float32 [128], replicated, may hold values from 0.25 to 1.75
- second_project: bfloat16 [128, 512], replicated, may hold values from -0.5 to 0.5
- second_gate: bfloat16 [128, 128], replicated, may hold values from -0.5 to 0.5
- second_norm: float32 [128], replicated, may hold values from 0.25 to 1.75
- second_final: bfloat16 [128, 128], replicated, may hold values from -0.5 to 0.5
Outputs:
- pair_output: bfloat16 [768, 384, 128], P(('groups', 'dap'), ('chan', 'sub')), parts along dimension 0
There are 2 independent parts, one for each index of `groups`. A program takes and returns all parts, laid end to end along the dimension named above; an argument that names none is the same for every part. Nothing has to cross between parts.
All inputs are finite; a program needn't handle non-finite values.
Results may differ from a plain program's by a relative error of at most 0.013.
Values may be sent and summed in bfloat16 or wider, within the bound.
A program may use at most 64 MiB of HBM per device.

v0:
```python
import jax
import jax.numpy as jnp
from jax import lax
from jax.sharding import PartitionSpec as P

epsilon = 1e-05


def layer_norm(values, norm_gain, reduce_axis):
    average = jnp.mean(values, axis=reduce_axis, keepdims=True)
    centred = values - average
    variance = jnp.mean(centred * centred, axis=reduce_axis, keepdims=True)
    return centred * lax.rsqrt(variance + epsilon) * norm_gain


def project_in(pair_state, norm_gain, project, gate_matrix):
    row_count, col_count, features = pair_state.shape
    flattened = pair_state.reshape(row_count * col_count, features).astype(jnp.float32)
    normed = layer_norm(flattened, norm_gain, 1).astype(jnp.bfloat16)
    projected = jnp.einsum("xc,cd->dx", normed, project, preferred_element_type=jnp.float32)
    left_part = jax.nn.sigmoid(projected[:features]) * projected[features : 2 * features]
    right_part = jax.nn.sigmoid(projected[2 * features : 3 * features]) * projected[3 * features :]
    left_part = left_part.astype(jnp.bfloat16).reshape(features, row_count, col_count)
    right_part = right_part.astype(jnp.bfloat16).reshape(features, row_count, col_count)
    gating = jax.nn.sigmoid(jnp.dot(normed, gate_matrix, preferred_element_type=jnp.float32))
    return (left_part, right_part, gating)


def finish(pair_state, mixture, gating, out_gain, final_matrix):
    features = mixture.shape[0]
    flattened = mixture.reshape(features, -1).astype(jnp.float32)
    normed = layer_norm(flattened, out_gain[:, None], 0).astype(jnp.bfloat16)
    update = jnp.einsum("cx,cd->xd", normed, final_matrix, preferred_element_type=jnp.float32)
    result = pair_state.reshape(-1, features).astype(jnp.float32) + gating * update
    return result.astype(jnp.bfloat16).reshape(pair_state.shape)


def shards(
    pair_input,
    first_gain,
    first_project,
    first_gate,
    first_norm,
    first_final,
    second_gain,
    second_project,
    second_gate,
    second_norm,
    second_final,
):
    left_part, right_part, gating = project_in(pair_input, first_gain, first_project, first_gate)
    left_part, right_part = (
        lax.all_to_all(left_part, ("chan", "sub"), split_axis=0, concat_axis=2, tiled=True),
        lax.all_to_all(right_part, ("chan", "sub"), split_axis=0, concat_axis=2, tiled=True),
    )
    mixture = jnp.einsum(
        "cik,cjk->cij",
        left_part,
        lax.all_gather(right_part, "dap", axis=1, tiled=True),
        preferred_element_type=jnp.float32,
    ).astype(jnp.bfloat16)
    mixture = lax.all_to_all(mixture, ("chan", "sub"), split_axis=2, concat_axis=0, tiled=True)
    middle = finish(pair_input, mixture, gating, first_norm, first_final)
    left_part, right_part, gating = project_in(middle, second_gain, second_project, second_gate)
    left_part, right_part = (
        lax.all_to_all(left_part, ("chan", "sub"), split_axis=0, concat_axis=2, tiled=True),
        lax.all_to_all(right_part, ("chan", "sub"), split_axis=0, concat_axis=2, tiled=True),
    )
    turned = lax.all_to_all(left_part, "dap", split_axis=2, concat_axis=1, tiled=True)
    mixture = jnp.einsum(
        "cki,ckj->cij",
        turned,
        lax.all_gather(right_part, "dap", axis=1, tiled=True),
        preferred_element_type=jnp.float32,
    )
    mixture = lax.all_to_all(
        mixture.astype(jnp.bfloat16), ("chan", "sub"), split_axis=2, concat_axis=0, tiled=True
    )
    return finish(middle, mixture, gating, second_norm, second_final)


def solution(mesh):
    placed = (
        P(("groups", "dap"), ("chan", "sub"), None),
        P(),
        P(),
        P(),
        P(),
        P(),
        P(),
        P(),
        P(),
        P(),
        P(),
    )
    return jax.shard_map(
        shards,
        mesh=mesh,
        in_specs=placed,
        out_specs=P(("groups", "dap"), ("chan", "sub"), None),
        check_vma=False,
    )
```

profile of v0, /device:TPU:0, one launch (start us, length us, event | category | flops | bytes accessed | tf_op | source)
XLA Modules:
  0.0 717.0 jit_solution(18188985698345366559)
XLA Ops:
  13.9 4.9 fusion.29
  26.8 4.8 copy.28
  31.6 41.2 %all_to_all.108 = bf16[128,96,96]{2,1,0:T(8,128)(2,1)S(1)} all-to-all(bf16[128,96,96]{2,1,0:T(8,128)(2,1)} %copy.28), channel_id=1, replica_groups=mesh['groups'=2,'dap'=4,'chan'=2,'sub'=2] {'chan','sub'}, dimensions={0} | all-to-all | bytes 4718592 | tf_op jit(solution)/shard_map/all_to_all | solution.py:54
  76.9 5.9 all_to_all.86
  82.9 4.8 copy.26
  87.6 41.0 %all_to_all.109 = bf16[128,96,96]{2,1,0:T(8,128)(2,1)S(1)} all-to-all(bf16[128,96,96]{2,1,0:T(8,128)(2,1)} %copy.26), channel_id=1, replica_groups=mesh['groups'=2,'dap'=4,'chan'=2,'sub'=2] {'chan','sub'}, dimensions={0} | all-to-all | bytes 4718592 | tf_op jit(solution)/shard_map/all_to_all | solution.py:53
  132.7 5.9 all_to_all.82
  138.6 112.3 %all-gather.3.cloned.1.call-done = bf16[32,384,384]{2,1,0:T(8,128)(2,1)} async-done(((bf16[32,96,384]{2,1,0:T(8,128)(2,1)}), bf16[32,384,384]{2,1,0:T(8,128)(2,1)}) %all-gather.3.cloned.1.call-update) | async-done | bytes 9437200 | tf_op jit(solution)/shard_map/all_gather | solution.py:59
  251.0 9.1 %convolution_convert_fusion.1 = bf16[32,96,384]{2,1,0:T(8,128)(2,1)} fusion(bf16[32,96,384]{2,1,0:T(8,128)(2,1)} %all_to_all.82, bf16[32,384,384]{2,1,0:T(8,128)(2,1)} %all-gather.3.cloned.1.call-done), kind=kOutput, calls=%fused_computation.61 | convolution fusion | flops 907149312 | bytes 14155776 | tf_op jit(solution)/shard_map/cik,cjk->cij/dot_general | solution.py:56
  260.0 5.0 copy.30
  265.0 4.7 all-to-all-start.2
  269.8 5.2 fusion.9
  275.0 31.7 %all-to-all-done.2 = bf16[32,96,384]{1,0,2:T(8,128)(2,1)} async-done(((bf16[32,96,384]{1,0,2:T(8,128)(2,1)}), bf16[32,96,384]{1,0,2:T(8,128)(2,1)}, u32[]{:S(2)}, u32[]{:S(2)}) %all-to-all-start.2) | async-done | bytes 2359328 | tf_op jit(solution)/shard_map/all_to_all | solution.py:62
  306.7 6.9 copy.31
  319.3 7.2 %reshape.153 = f32[128,9216]{1,0:T(8,128)} reshape(f32[4,32,96,96]{3,2,1,0:T(8,128)} %bitcast.64) | data formatting | bytes 9437184 | tf_op jit(solution)/shard_map/convert_element_type | solution.py:31
  326.5 5.9 fusion.36
  341.4 4.7 copy.37
  346.2 40.8 %all_to_all.110 = bf16[128,96,96]{2,1,0:T(8,128)(2,1)S(1)} all-to-all(bf16[128,96,96]{2,1,0:T(8,128)(2,1)} %copy.37), channel_id=1, replica_groups=mesh['groups'=2,'dap'=4,'chan'=2,'sub'=2] {'chan','sub'}, dimensions={0} | all-to-all | bytes 4718592 | tf_op jit(solution)/shard_map/all_to_all | solution.py:67
  391.0 5.9 all_to_all.99
  400.2 42.3 %all_to_all.111 = bf16[128,96,96]{2,1,0:T(8,128)(2,1)} all-to-all(bf16[128,96,96]{2,1,0:T(8,128)(2,1)} %copy.32), channel_id=1, replica_groups=mesh['groups'=2,'dap'=4,'chan'=2,'sub'=2] {'chan','sub'}, dimensions={0} | all-to-all | bytes 4718592 | tf_op jit(solution)/shard_map/all_to_all | solution.py:66
  442.5 6.6 copy.41
  449.1 159.5 %all_to_all.112 = bf16[32,96,384]{1,0,2:T(8,128)(2,1)S(1)} all-to-all(bf16[32,96,384]{1,0,2:T(8,128)(2,1)} %bitcast.71), channel_id=1, replica_groups=mesh['groups'=2,'dap'=4,'chan'=2,'sub'=2] {'dap'}, dimensions={2} | all-to-all | bytes 4718592 | tf_op jit(solution)/shard_map/all_to_all | solution.py:69
  612.6 5.0 all_to_all.95
  617.6 10.7 %all-gather.5.cloned.1.call-done = bf16[32,384,384]{2,1,0:T(8,128)(2,1)} async-done(((bf16[32,96,384]{2,1,0:T(8,128)(2,1)}), bf16[32,384,384]{2,1,0:T(8,128)(2,1)}) %all-gather.5.cloned.1.call-update) | async-done | bytes 9437200 | tf_op jit(solution)/shard_map/all_gather | solution.py:73
  628.3 7.0 convolution_convert_fusion
  635.3 5.0 copy.39
  640.4 4.8 all-to-all-start.6
  645.2 6.7 fusion.10
  651.9 30.3 %all-to-all-done.6 = bf16[32,96,384]{1,0,2:T(8,128)(2,1)} async-done(((bf16[32,96,384]{1,0,2:T(8,128)(2,1)}), bf16[32,96,384]{1,0,2:T(8,128)(2,1)}, u32[]{:S(2)}, u32[]{:S(2)}) %all-to-all-start.6) | async-done | bytes 2359328 | tf_op jit(solution)/shard_map/all_to_all | solution.py:76
  682.2 6.9 copy.40
  694.8 7.2 %reshape.154 = f32[128,9216]{1,0:T(8,128)} reshape(f32[4,32,96,96]{3,2,1,0:T(8,128)} %bitcast.65) | data formatting | bytes 9437184 | tf_op jit(solution)/shard_map/convert_element_type | solution.py:31
  702.0 8.0 %fusion.7 = bf16[9216,128]{1,0:T(8,128)(2,1)} fusion(f32[9216,128]{1,0:T(8,128)} %copy-done.4, f32[9216,128]{1,0:T(8,128)} %fusion.10, bf16[128,128]{1,0:T(8,128)(2,1)S(1)} %copy-done.9, f32[128,9216]{1,0:T(8,128)} %reshape.154, f32[128]{0:T(128)S(1)} %copy-done.13, f32[9216]{0:T(1024)S(1)} %rsqrt.47, f32[9216]{0:T(1024)S(1)} %div.63), kind=kOutput, calls=%fused_computation.13 | convolution fusion | flops 310247424 | bytes 16622080 | tf_op jit(solution)/shard_map/cx,cd->xd/dot_general | solution.py:33
  (66 shorter events, 55.0 us)
Async XLA Ops:
  6.5 13.7 %copy-start = (bf16[128,512]{1,0:T(8,128)(2,1)S(1)}, bf16[128,512]{1,0:T(8,128)(2,1)}, u32[]{:S(2)}) copy-start(bf16[128,512]{1,0:T(8,128)(2,1)} %param.13) | copy-start | bytes 393220
  6.5 7.3 %copy-start.5 = (bf16[96,96,128]{2,1,0:T(8,128)(2,1)S(1)}, bf16[96,96,128]{2,1,0:T(8,128)(2,1)}, u32[]{:S(2)}) copy-start(bf16[96,96,128]{2,1,0:T(8,128)(2,1)} %param.11) | copy-start | bytes 7077892
  6.5 7.3 %copy-start.12 = (f32[128]{0:T(128)S(1)}, f32[128]{0:T(128)}, u32[]{:S(2)}) copy-start(f32[128]{0:T(128)} %param.12) | copy-start | bytes 1540
  6.5 244.4 %all-gather.3.cloned.1.call-start = ((), (), s32[]{:S(2)}) async-start(), calls=%async_computation.7 | async-start | bytes 11796480 | tf_op jit(solution)/shard_map/all_gather | solution.py:59
  18.9 1.4 copy-start.6
  260.0 9.7 %copy-start.14 = (bf16[128,128]{1,0:T(8,128)(2,1)S(1)}, bf16[128,128]{1,0:T(8,128)(2,1)}, u32[]{:S(2)}) copy-start(bf16[128,128]{1,0:T(8,128)(2,1)} %param.14) | copy-start | bytes 98308
  265.0 41.7 %all-to-all-start.2 = ((bf16[32,96,384]{1,0,2:T(8,128)(2,1)}), bf16[32,96,384]{1,0,2:T(8,128)(2,1)}, u32[]{:S(2)}, u32[]{:S(2)}) async-start(bf16[32,96,384]{1,0,2:T(8,128)(2,1)} %copy.30), calls=%async_computation.2 | async-start | bytes 6291456 | tf_op jit(solution)/shard_map/all_to_all | solution.py:62
  269.7 358.6 %all-gather.5.cloned.1.call-start = ((), (), s32[]{:S(2)}) async-start(), calls=%async_computation.8 | async-start | bytes 11796480 | tf_op jit(solution)/shard_map/all_gather | solution.py:73
  313.6 4.6 copy-start.2
  319.3 7.2 %copy-start.8 = (bf16[128,128]{1,0:T(8,128)(2,1)S(1)}, bf16[128,128]{1,0:T(8,128)(2,1)}, u32[]{:S(2)}) copy-start(bf16[128,128]{1,0:T(8,128)(2,1)} %param.16) | copy-start | bytes 98308
  319.3 7.2 %copy-start.11 = (f32[128]{0:T(128)S(1)}, f32[128]{0:T(128)}, u32[]{:S(2)}) copy-start(f32[128]{0:T(128)} %param.15) | copy-start | bytes 1540
  332.4 5.5 copy-start.4
  332.4 2.8 copy-start.7
  332.4 2.8 copy-start.10
  635.3 9.9 %copy-start.15 = (bf16[128,128]{1,0:T(8,128)(2,1)S(1)}, bf16[128,128]{1,0:T(8,128)(2,1)}, u32[]{:S(2)}) copy-start(bf16[128,128]{1,0:T(8,128)(2,1)} %param.19) | copy-start | bytes 98308
  640.4 41.8 %all-to-all-start.6 = ((bf16[32,96,384]{1,0,2:T(8,128)(2,1)}), bf16[32,96,384]{1,0,2:T(8,128)(2,1)}, u32[]{:S(2)}, u32[]{:S(2)}) async-start(bf16[32,96,384]{1,0,2:T(8,128)(2,1)} %copy.39), calls=%async_computation.6 | async-start | bytes 6291456 | tf_op jit(solution)/shard_map/all_to_all | solution.py:76
  689.1 4.6 copy-start.3
  694.8 7.2 %copy-start.9 = (bf16[128,128]{1,0:T(8,128)(2,1)S(1)}, bf16[128,128]{1,0:T(8,128)(2,1)}, u32[]{:S(2)}) copy-start(bf16[128,128]{1,0:T(8,128)(2,1)} %param.21) | copy-start | bytes 98308
  694.8 7.2 %copy-start.13 = (f32[128]{0:T(128)S(1)}, f32[128]{0:T(128)}, u32[]{:S(2)}) copy-start(f32[128]{0:T(128)} %param.20) | copy-start | bytes 1540
  694.8 15.2 %copy-start.1 = (bf16[128,512]{1,0:T(8,128)(2,1)S(1)}, bf16[128,512]{1,0:T(8,128)(2,1)}, u32[]{:S(2)}) copy-start(bf16[128,512]{1,0:T(8,128)(2,1)} %param.13) | copy-start | bytes 393220
Sparse Core Ops, SparseCore 0:
  83.0 167.9 all-gather.2
  397.1 231.1 all-gather.4
where the time goes:
time: 727 us; the launch traced here: 717 us
  blocking collectives  325 us (45%)
  waiting for transfers between devices  185 us (25%)
  local copies, waits for them, and re-layouts  106 us (15%)
  matrix products  47.1 us (6%)
  other arithmetic  30.8 us (4%)
  between operations  13.9 us (2%)
  starting transfers between devices  9.54 us (1%)
    all_to_all x1, blocking collectives, shards(): lax.all_to_all(left_part, 'dap', split_axis=2, concat_axis=1, tiled=True)  159 us
    all_gather x2, waiting for transfers between devices, shards(): lax.all_gather(right_part, 'dap', axis=1, tiled=True)  123 us
    all_to_all x2, blocking collectives, shards(): lax.all_to_all(left_part, ('chan', 'sub'), split_axis=0, concat_axis=2, t...  83.4 us
    all_to_all x2, blocking collectives, shards(): lax.all_to_all(right_part, ('chan', 'sub'), split_axis=0, concat_axis=2,...  82 us
    all_to_all x1, waiting for transfers between devices, shards(): lax.all_to_all(mixture, ('chan', 'sub'), split_axis=2, concat_axis=0, til...  31.7 us
    all_to_all x1, waiting for transfers between devices, shards(): lax.all_to_all(mixture.astype(jnp.bfloat16), ('chan', 'sub'), split_axis=...  30.3 us
    convert_element_type x4, local copies, waits for them, and re-layouts, finish(): flattened = mixture.reshape(features, -1).astype(jnp.float32)  28.1 us
    all_to_all x4, local copies, waits for them, and re-layouts, shards(): lax.all_to_all(right_part, ('chan', 'sub'), split_axis=0, concat_axis=2,...  20 us
  transfers between devices with their start and end apart: 4, of which 4 were waited for; matrix products, arithmetic and copies ran while one was open for 5% of the time, Pallas kernels for 0%

commit v1 on v0

--- a/solution.py
+++ b/solution.py
@@ -1,6 +1,10 @@
+import functools
+
 import jax
 import jax.numpy as jnp
 from jax import lax
+from jax.experimental import pallas as pl
+from jax.experimental.pallas import tpu as pltpu
 from jax.sharding import PartitionSpec as P
 
 epsilon = 1e-05
@@ -33,6 +37,164 @@
     update = jnp.einsum("cx,cd->xd", normed, final_matrix, preferred_element_type=jnp.float32)
     result = pair_state.reshape(-1, features).astype(jnp.float32) + gating * update
     return result.astype(jnp.bfloat16).reshape(pair_state.shape)
+
+
+def exchange_kernel(plan, sizes, *refs):
+    halves, inner, chans, subs = sizes
+    cols = chans * subs
+    block = inner * cols
+    count = len(plan)
+    sources, targets = refs[:count], refs[count : 2 * count]
+    sems = refs[2 * count : 5 * count]
+    row = lax.axis_index("dap")
+    col = lax.axis_index("chan") * subs + lax.axis_index("sub")
+    mine = lax.rem(row, inner) * cols + col
+    half = row // inner
+    whole = halves * block
+    me = row * cols + col
+
+    def place(q):
+        owner_row, owner_col = q // cols, lax.rem(q, cols)
+        return {"dap": owner_row, "chan": owner_col // subs, "sub": lax.rem(owner_col, subs)}
+
+    barrier = pltpu.get_barrier_semaphore()
+    everyone = any(spans for _, spans in plan)
+    reach = whole if everyone else block
+    for off in range(1, reach):
+        q = lax.rem(me + off, whole) if everyone else half * block + lax.rem(mine + off, block)
+        pl.semaphore_signal(barrier, inc=1, device_id=place(q), device_id_type=pl.DeviceIdType.MESH)
+    pl.semaphore_wait(barrier, reach - 1)
+
+    started = []
+    for off in range(0, reach):
+        for (varies, spans), source, target, (sent, got, kept) in zip(
+            plan, sources, targets, [sems[3 * n : 3 * n + 3] for n in range(count)]
+        ):
+            if spans:
+                q = lax.rem(me + off, whole)
+                slot, back = me, lax.rem(me - off + whole, whole)
+            elif off < block:
+                q = half * block + lax.rem(mine + off, block)
+                slot, back = mine, lax.rem(mine - off + block, block)
+            else:
+                continue
+            piece = source.at[q if varies else lax.rem(q, block)]
+            if off == 0:
+                copy = pltpu.make_async_copy(piece, target.at[slot], kept)
+                copy.start()
+                started.append((copy, None))
+                continue
+            copy = pltpu.make_async_remote_copy(
+                src_ref=piece,
+                dst_ref=target.at[slot],
+                send_sem=sent.at[off],
+                recv_sem=got.at[off],
+                device_id=place(q),
+                device_id_type=pl.DeviceIdType.MESH,
+            )
+            copy.start()
+            arriving = pltpu.make_async_remote_copy(
+                src_ref=piece,
+                dst_ref=target.at[back],
+                send_sem=sent.at[off],
+                recv_sem=got.at[off],
+                device_id=place(q),
+                device_id_type=pl.DeviceIdType.MESH,
+            )
+            started.append((copy, arriving))
+    for copy, arriving in started:
+        if arriving is None:
+            copy.wait()
+        else:
+            copy.wait_send()
+            arriving.wait_recv()
+
+
+def exchange(plan, sizes, number, *arrays):
+    halves, inner, chans, subs = sizes
+    block = inner * chans * subs
+    shapes, sems = [], []
+    for (varies, spans), array in zip(plan, arrays):
+        slots = halves * block if spans else block
+        shapes.append(jax.ShapeDtypeStruct((slots,) + array.shape[1:], array.dtype))
+        sems += [
+            pltpu.SemaphoreType.DMA((slots,)),
+            pltpu.SemaphoreType.DMA((slots,)),
+            pltpu.SemaphoreType.DMA,
+        ]
+    return pl.pallas_call(
+        functools.partial(exchange_kernel, plan, sizes),
+        out_shape=shapes,
+        in_specs=[pl.BlockSpec(memory_space=pl.ANY)] * len(arrays),
+        out_specs=[pl.BlockSpec(memory_space=pl.ANY)] * len(arrays),
+        scratch_shapes=sems,
+        compiler_params=pltpu.CompilerParams(collective_id=number, has_side_effects=True),
+    )(*arrays)
+
+
+def direct_shards(
+    sizes,
+    pair_input,
+    first_gain,
+    first_project,
+    first_gate,
+    first_norm,
+    first_final,
+    second_gain,
+    second_project,
+    second_gate,
+    second_norm,
+    second_final,
+):
+    halves, inner, chans, subs = sizes
+    cols = chans * subs
+    block = inner * cols
+    rows, width, features = pair_input.shape
+    depth = features // block
+    span = rows * width
+
+    def blocks(part):
+        return part.reshape(block, depth, span)
+
+    def matrices(received, tall):
+        grid = received.reshape(tall, cols, depth, rows, width)
+        return grid.transpose(2, 0, 3, 1, 4).reshape(depth, tall * rows, cols * width)
+
+    def pieces(mixture, tall):
+        grid = mixture.reshape(depth, tall, rows, cols, width)
+        return grid.transpose(1, 3, 0, 2, 4).reshape(tall * cols, depth, span)
+
+    left, right, gating = project_in(pair_input, first_gain, first_project, first_gate)
+    left, right = exchange(
+        ((False, False), (False, True)), sizes, 0, blocks(left), blocks(right)
+    )
+    mixture = jnp.einsum(
+        "cik,cjk->cij",
+        matrices(left, inner),
+        matrices(right, halves * inner),
+        preferred_element_type=jnp.float32,
+    ).astype(jnp.bfloat16)
+    (mixture,) = exchange(
+        ((False, False),), sizes, 1, pieces(mixture, inner)
+    )
+    middle = finish(
+        pair_input, mixture.reshape(features, span), gating, first_norm, first_final
+    )
+    left, right, gating = project_in(middle, second_gain, second_project, second_gate)
+    left, right = exchange(
+        ((False, False), (False, False)), sizes, 2, blocks(left), blocks(right)
+    )
+    mixture = jnp.einsum(
+        "cki,ckj->cij",
+        matrices(left, inner),
+        matrices(right, inner),
+        preferred_element_type=jnp.float32,
+    ).astype(jnp.bfloat16)
+    (mixture,) = exchange(
+        ((True, True),), sizes, 3, pieces(mixture, halves * inner)
+    )
+    mixture = mixture.reshape(halves, features, span).astype(jnp.float32).sum(axis=0)
+    return finish(middle, mixture, gating, second_norm, second_final)
 
 
 def shards(
@@ -93,8 +255,19 @@
         P(),
         P(),
     )
+    chans, subs, rows = mesh.shape["chan"], mesh.shape["sub"], mesh.shape["dap"]
+    halves = 2 if rows % 2 == 0 else 1
+    sizes = (halves, rows // halves, chans, subs)
+    direct = functools.partial(direct_shards, sizes)
+
+    def chosen(pair_input, *weights):
+        features = pair_input.shape[2]
+        if features % (16 * (rows // halves) * chans * subs) == 0:
+            return direct(pair_input, *weights)
+        return shards(pair_input, *weights)
+
     return jax.shard_map(
-        shards,
+        chosen,
         mesh=mesh,
         in_specs=placed,
         out_specs=P(("groups", "dap"), ("chan", "sub"), None),

time: 727 us -> 511 us (0.70)
  the two profiles are of different devices: /device:TPU:0 before, /device:TPU:11 now
where the time goes in v1:
time: 511 us; the launch traced here: 503 us
  Pallas kernels  303 us (59%)
  local copies, waits for them, and re-layouts  131 us (26%)
  other arithmetic  41.7 us (8%)
  matrix products  26.8 us (5%)
    pallas_call x4, Pallas kernels, exchange(): pl.pallas_call(functools.partial(exchange_kernel, plan, sizes), out_shape...  303 us
    reshape x4, local copies, waits for them, and re-layouts, pieces(): grid = mixture.reshape(depth, tall, rows, cols, width)  29.9 us
    reshape x4, local copies, waits for them, and re-layouts, matrices(): grid.transpose(2, 0, 3, 1, 4).reshape(depth, tall * rows, cols * width)  28.8 us
    transpose x4, local copies, waits for them, and re-layouts, matrices(): grid.transpose(2, 0, 3, 1, 4).reshape(depth, tall * rows, cols * width)  27.7 us
    reshape x4, local copies, waits for them, and re-layouts, matrices(): grid = received.reshape(tall, cols, depth, rows, width)  25.4 us
    reshape x2, local copies, waits for them, and re-layouts, pieces(): return grid.transpose(1, 3, 0, 2, 4).reshape(tall * cols, depth, span)  18.8 us

profile of v1, /device:TPU:11, one launch (start us, length us, event | category | flops | bytes accessed | tf_op | source)
XLA Modules:
  0.0 502.8 jit_solution(14882232086865472025)
XLA Ops:
  2.8 4.4 multiply_reduce_fusion.3
  7.4 4.9 fusion.32
  15.0 3.9 fusion.19
  18.9 111.4 %shard_map.109 = (bf16[8,16,9216]{2,1,0:T(8,128)(2,1)}, bf16[16,16,9216]{2,1,0:T(8,128)(2,1)}) custom-call(bf16[8,16,9216]{2,1,0:T(8,128)(2,1)} %bitcast.69, bf16[8,16,9216]{2,1,0:T(8,128)(2,1)} %bitcast.68), custom_call_target="tpu_custom_call" | custom-call | tf_op jit(solution)/shard_map/pallas_call | solution.py:125
  130.4 10.2 %reshape.128 = bf16[4,4,16,96,96]{4,3,2,1,0:T(8,128)(2,1)} reshape(bf16[16,16,9216]{2,1,0:T(8,128)(2,1)} %get-tuple-element.10) | data formatting | bytes 9437184 | tf_op jit(solution)/shard_map/reshape | solution.py:160
  140.6 13.5 %copy.19 = bf16[16,4,96,4,96]{4,3,2,1,0:T(4,128)(2,1)} copy(bf16[16,4,96,4,96]{4,2,0,3,1:T(8,128)(2,1)} %bitcast.62) | data formatting | bytes 9437184 | tf_op jit(solution)/shard_map/transpose | solution.py:161
  154.1 10.8 %reshape.129 = bf16[16,384,384]{2,1,0:T(8,128)(2,1)} reshape(bf16[16,4,96,4,96]{4,3,2,1,0:T(4,128)(2,1)} %copy.19) | data formatting | bytes 9437184 | tf_op jit(solution)/shard_map/reshape | solution.py:161
  164.9 6.0 %reshape.126 = bf16[2,4,16,96,96]{4,3,2,1,0:T(8,128)(2,1)} reshape(bf16[8,16,9216]{2,1,0:T(8,128)(2,1)} %get-tuple-element.9) | data formatting | bytes 4718592 | tf_op jit(solution)/shard_map/reshape | solution.py:160
  170.9 6.1 %copy.18 = bf16[16,2,96,4,96]{4,3,2,1,0:T(4,128)(2,1)} copy(bf16[16,2,96,4,96]{4,2,0,3,1:T(8,128)(2,1)} %bitcast.64) | data formatting | bytes 4718592 | tf_op jit(solution)/shard_map/transpose | solution.py:161
  177.0 5.9 %reshape.127 = bf16[16,192,384]{2,1,0:T(8,128)(2,1)} reshape(bf16[16,2,96,4,96]{4,3,2,1,0:T(4,128)(2,1)} %copy.18) | data formatting | bytes 4718592 | tf_op jit(solution)/shard_map/reshape | solution.py:161
  182.9 6.4 %convolution_convert_fusion.1 = bf16[16,192,384]{2,1,0:T(8,128)(2,1)} fusion(bf16[16,192,384]{2,1,0:T(8,128)(2,1)} %reshape.127, bf16[16,384,384]{2,1,0:T(8,128)(2,1)} %reshape.129), kind=kOutput, calls=%fused_computation.65 | convolution fusion | flops 907149312 | bytes 9437184 | tf_op jit(solution)/shard_map/cik,cjk->cij/dot_general | solution.py:171
  189.4 6.9 %reshape.130 = bf16[16,2,96,4,96]{4,3,2,1,0:T(4,128)(2,1)} reshape(bf16[16,192,384]{2,1,0:T(8,128)(2,1)} %convolution_convert_fusion.1) | data formatting | bytes 4718592 | tf_op jit(solution)/shard_map/reshape | solution.py:164
  196.2 4.1 copy.27
  200.3 6.9 %reshape.131.refs_0_ = bf16[8,16,9216]{2,1,0:T(8,128)(2,1)} reshape(bf16[2,4,16,96,96]{4,3,2,1,0:T(8,128)(2,1)} %bitcast.65) | data formatting | bytes 4718592 | tf_op jit(solution)/shard_map/reshape | solution.py:165
  207.2 29.9 %shard_map.110 = bf16[8,16,9216]{2,1,0:T(8,128)(2,1)} custom-call(bf16[8,16,9216]{2,1,0:T(8,128)(2,1)} %reshape.131.refs_0_), custom_call_target="tpu_custom_call" | custom-call | tf_op jit(solution)/shard_map/pallas_call | solution.py:125
  248.8 2.9 convolution_bitcast_fusion
  251.7 3.9 fusion.11
  255.6 54.5 %shard_map.111 = (bf16[8,16,9216]{2,1,0:T(8,128)(2,1)}, bf16[8,16,9216]{2,1,0:T(8,128)(2,1)}) custom-call(bf16[8,16,9216]{2,1,0:T(8,128)(2,1)} %bitcast.71, bf16[8,16,9216]{2,1,0:T(8,128)(2,1)} %bitcast.70), custom_call_target="tpu_custom_call" | custom-call | tf_op jit(solution)/shard_map/pallas_call | solution.py:125
  310.1 4.7 reshape.132
  314.8 4.1 copy.21
  318.9 5.9 %reshape.133 = bf16[16,192,384]{2,1,0:T(8,128)(2,1)} reshape(bf16[16,2,96,4,96]{4,3,2,1,0:T(4,128)(2,1)} %copy.21) | data formatting | bytes 4718592 | tf_op jit(solution)/shard_map/reshape | solution.py:161
  324.8 4.5 reshape.134
  329.3 4.1 copy.22
  333.4 6.1 %reshape.135 = bf16[16,192,384]{2,1,0:T(8,128)(2,1)} reshape(bf16[16,2,96,4,96]{4,3,2,1,0:T(4,128)(2,1)} %copy.22) | data formatting | bytes 4718592 | tf_op jit(solution)/shard_map/reshape | solution.py:161
  339.5 5.8 %convolution_convert_fusion = bf16[16,384,384]{2,1,0:T(8,128)(2,1)} fusion(bf16[16,192,384]{2,1,0:T(8,128)(2,1)S(1)} %copy-done.7, bf16[16,192,384]{2,1,0:T(8,128)(2,1)} %reshape.135), kind=kOutput, calls=%fused_computation.59 | convolution fusion | flops 908328960 | bytes 9437184 | tf_op jit(solution)/shard_map/cki,ckj->cij/dot_general | solution.py:187
  345.3 12.3 %reshape.136 = bf16[16,4,96,4,96]{4,3,2,1,0:T(4,128)(2,1)} reshape(bf16[16,384,384]{2,1,0:T(8,128)(2,1)} %convolution_convert_fusion) | data formatting | bytes 9437184 | tf_op jit(solution)/shard_map/reshape | solution.py:164
  357.6 6.6 %copy.26 = bf16[16,4,96,4,96]{4,2,0,3,1:T(8,128)(2,1)} copy(bf16[16,4,96,4,96]{4,3,2,1,0:T(4,128)(2,1)} %reshape.136) | data formatting | bytes 9437184 | tf_op jit(solution)/shard_map/reshape | solution.py:164
  364.2 11.9 %reshape.137.refs_0_ = bf16[16,16,9216]{2,1,0:T(8,128)(2,1)} reshape(bf16[4,4,16,96,96]{4,3,2,1,0:T(8,128)(2,1)} %bitcast.63) | data formatting | bytes 9437184 | tf_op jit(solution)/shard_map/reshape | solution.py:165
  376.1 106.6 %shard_map.112 = bf16[16,16,9216]{2,1,0:T(8,128)(2,1)} custom-call(bf16[16,16,9216]{2,1,0:T(8,128)(2,1)} %reshape.137.refs_0_), custom_call_target="tpu_custom_call" | custom-call | tf_op jit(solution)/shard_map/pallas_call | solution.py:125
  482.8 7.2 %convert_element_type.94 = f32[16,16,9216]{2,1,0:T(8,128)} convert(bf16[16,16,9216]{2,1,0:T(8,128)(2,1)} %shard_map.112) | non-fusion elementwise | flops 2359296 | bytes 14155776 | tf_op jit(solution)/shard_map/convert_element_type | solution.py:196
  490.1 5.2 %bitcast_reduce_fusion = f32[128,9216]{1,0:T(8,128)S(1)} fusion(f32[2,128,9216]{2,1,0:T(8,128)} %bitcast.60), kind=kLoop, calls=%fused_computation.17 | loop fusion | flops 1179648 | bytes 14155776 | tf_op jit(solution)/shard_map/reduce_sum | solution.py:196
  499.4 3.0 fusion.7
  (65 shorter events, 21.2 us)
Async XLA Ops:
  0.0 12.3 %copy-start = (bf16[128,512]{1,0:T(8,128)(2,1)S(1)}, bf16[128,512]{1,0:T(8,128)(2,1)}, u32[]{:S(2)}) copy-start(bf16[128,512]{1,0:T(8,128)(2,1)} %param.13) | copy-start | bytes 393220
  0.0 7.3 %copy-start.4 = (bf16[96,96,128]{2,1,0:T(8,128)(2,1)S(1)}, bf16[96,96,128]{2,1,0:T(8,128)(2,1)}, u32[]{:S(2)}) copy-start(bf16[96,96,128]{2,1,0:T(8,128)(2,1)} %param.11) | copy-start | bytes 7077892
  0.0 7.3 %copy-start.12 = (f32[128]{0:T(128)S(1)}, f32[128]{0:T(128)}, u32[]{:S(2)}) copy-start(f32[128]{0:T(128)} %param.12) | copy-start | bytes 1540
  12.3 2.7 copy-start.5
  207.2 34.6 %copy-start.13 = (f32[128]{0:T(128)S(1)}, f32[128]{0:T(128)}, u32[]{:S(2)}) copy-start(f32[128]{0:T(128)} %param.15) | copy-start | bytes 1540
  237.1 4.6 copy-start.3
  237.1 5.3 %copy-start.6 = (bf16[9216,128]{1,0:T(8,128)(2,1)S(1)}, bf16[9216,128]{1,0:T(8,128)(2,1)}, u32[]{:S(2)}) copy-start(bf16[9216,128]{1,0:T(8,128)(2,1)} %copy-done.5) | copy-start | bytes 7077892
  237.1 5.3 %copy-start.15 = (bf16[128,128]{1,0:T(8,128)(2,1)S(1)}, bf16[128,128]{1,0:T(8,128)(2,1)}, u32[]{:S(2)}) copy-start(bf16[128,128]{1,0:T(8,128)(2,1)} %param.14) | copy-start | bytes 98308
  242.5 1.4 copy-start.9
  246.0 5.7 %copy-start.2 = (f32[9216,128]{1,0:T(8,128)}, f32[9216,128]{1,0:T(8,128)S(1)}, u32[]{:S(2)}) copy-start(f32[9216,128]{1,0:T(8,128)S(1)} %get-tuple-element.18) | copy-start | bytes 14155780
  246.0 2.8 copy-start.8
  246.0 2.8 copy-start.11
  333.4 6.1 %copy-start.7 = (bf16[16,192,384]{2,1,0:T(8,128)(2,1)S(1)}, bf16[16,192,384]{2,1,0:T(8,128)(2,1)}, u32[]{:S(2)}) copy-start(bf16[16,192,384]{2,1,0:T(8,128)(2,1)} %reshape.133) | copy-start | bytes 7077892
  482.8 12.5 %slice-start.2 = ((s8[4718592]{0:T(1024)(128)(4,1)}), s8[4194304]{0:T(1024)(128)(4,1)S(1)}, s32[]{:S(2)}) async-start(s8[4718592]{0:T(1024)(128)(4,1)} %bitcast.58), calls=%async_computation.2 | async-start | bytes 8388608
  490.0 5.2 %slice-start.3 = ((s8[4718592]{0:T(1024)(128)(4,1)}), s8[524288]{0:T(1024)(128)(4,1)S(1)}, s32[]{:S(2)}) async-start(s8[4718592]{0:T(1024)(128)(4,1)} %bitcast.58), calls=%async_computation.3 | async-start | bytes 1048576
  490.1 6.6 %slice-start = ((s8[4718592]{0:T(1024)(128)(4,1)}), s8[4194304]{0:T(1024)(128)(4,1)S(1)}, s32[]{:S(2)}) async-start(s8[4718592]{0:T(1024)(128)(4,1)} %bitcast.56), calls=%async_computation | async-start | bytes 8388608
  490.1 6.6 %slice-start.1 = ((s8[4718592]{0:T(1024)(128)(4,1)}), s8[524288]{0:T(1024)(128)(4,1)S(1)}, s32[]{:S(2)}) async-start(s8[4718592]{0:T(1024)(128)(4,1)} %bitcast.56), calls=%async_computation.1 | async-start | bytes 1048576
  495.3 1.4 copy-start.16
  496.7 2.7 copy-start.10
  496.7 2.7 copy-start.14
  496.7 5.7 %copy-start.1 = (bf16[128,512]{1,0:T(8,128)(2,1)S(1)}, bf16[128,512]{1,0:T(8,128)(2,1)}, u32[]{:S(2)}) copy-start(bf16[128,512]{1,0:T(8,128)(2,1)} %param.13) | copy-start | bytes 393220

commit v2 on v1

--- a/solution.py
+++ b/solution.py
@@ -132,6 +132,57 @@
     )(*arrays)
 
 
+def product_kernel(turned, left_ref, right_ref, out_ref):
+    left_tall, cols, depth, rows, width = left_ref.shape
+    right_tall = right_ref.shape[0]
+
+    def matrix(ref, tall, channel):
+        return jnp.concatenate(
+            [
+                jnp.concatenate([ref[t, x, channel] for x in range(cols)], axis=1)
+                for t in range(tall)
+            ],
+            axis=0,
+        )
+
+    side = 0 if turned else 1
+    for channel in range(depth):
+        mixed = lax.dot_general(
+            matrix(left_ref, left_tall, channel),
+            matrix(right_ref, right_tall, channel),
+            (((side,), (side,)), ((), ())),
+            preferred_element_type=jnp.float32,
+        ).astype(out_ref.dtype)
+        for t in range(out_ref.shape[0]):
+            for x in range(cols):
+                out_ref[t, x, channel] = mixed[
+                    t * rows : (t + 1) * rows, x * width : (x + 1) * width
+                ]
+
+
+def product(turned, left, right):
+    left_tall, cols, depth, rows, width = left.shape
+    right_tall = right.shape[0]
+    tall = cols if turned else left_tall
+    step = 4 if depth % 4 == 0 else 1
+
+    def spec(high):
+        return pl.BlockSpec((high, cols, step, rows, width), lambda n: (0, 0, n, 0, 0))
+
+    flops = 2 * depth * (tall * rows) * (cols * width) * (left_tall * rows if turned else cols * width)
+    return pl.pallas_call(
+        functools.partial(product_kernel, turned),
+        out_shape=jax.ShapeDtypeStruct((tall, cols, depth, rows, width), jnp.bfloat16),
+        grid=(depth // step,),
+        in_specs=[spec(left_tall), spec(right_tall)],
+        out_specs=spec(tall),
+        compiler_params=pltpu.CompilerParams(vmem_limit_bytes=40 * 2**20),
+        cost_estimate=pl.CostEstimate(
+            flops=flops, bytes_accessed=2 * (left.size + right.size), transcendentals=0
+        ),
+    )(left, right)
+
+
 def direct_shards(
     sizes,
     pair_input,
@@ -154,29 +205,17 @@
     span = rows * width
 
     def blocks(part):
-        return part.reshape(block, depth, span)
-
-    def matrices(received, tall):
-        grid = received.reshape(tall, cols, depth, rows, width)
-        return grid.transpose(2, 0, 3, 1, 4).reshape(depth, tall * rows, cols * width)
-
-    def pieces(mixture, tall):
-        grid = mixture.reshape(depth, tall, rows, cols, width)
-        return grid.transpose(1, 3, 0, 2, 4).reshape(tall * cols, depth, span)
+        return part.reshape(-1, depth, span)
+
+    def grid(received, tall):
+        return received.reshape(tall, cols, depth, rows, width)
 
     left, right, gating = project_in(pair_input, first_gain, first_project, first_gate)
     left, right = exchange(
         ((False, False), (False, True)), sizes, 0, blocks(left), blocks(right)
     )
-    mixture = jnp.einsum(
-        "cik,cjk->cij",
-        matrices(left, inner),
-        matrices(right, halves * inner),
-        preferred_element_type=jnp.float32,
-    ).astype(jnp.bfloat16)
-    (mixture,) = exchange(
-        ((False, False),), sizes, 1, pieces(mixture, inner)
-    )
+    mixture = product(False, grid(left, inner), grid(right, halves * inner))
+    (mixture,) = exchange(((False, False),), sizes, 1, blocks(mixture))
     middle = finish(
         pair_input, mixture.reshape(features, span), gating, first_norm, first_final
     )
@@ -184,15 +223,8 @@
     left, right = exchange(
         ((False, False), (False, False)), sizes, 2, blocks(left), blocks(right)
     )
-    mixture = jnp.einsum(
-        "cki,ckj->cij",
-        matrices(left, inner),
-        matrices(right, inner),
-        preferred_element_type=jnp.float32,
-    ).astype(jnp.bfloat16)
-    (mixture,) = exchange(
-        ((True, True),), sizes, 3, pieces(mixture, halves * inner)
-    )
+    mixture = product(True, grid(left, inner), grid(right, inner))
+    (mixture,) = exchange(((True, True),), sizes, 3, blocks(mixture))
     mixture = mixture.reshape(halves, features, span).astype(jnp.float32).sum(axis=0)
     return finish(middle, mixture, gating, second_norm, second_final)
 
@@ -262,7 +294,8 @@
 
     def chosen(pair_input, *weights):
         features = pair_input.shape[2]
-        if features % (16 * (rows // halves) * chans * subs) == 0:
+        square = pair_input.shape[0] == pair_input.shape[1] and rows == chans * subs
+        if square and features % (16 * (rows // halves) * chans * subs) == 0:
             return direct(pair_input, *weights)
         return shards(pair_input, *weights)
 

time: 511 us -> 428 us (0.84); the launches traced: 503 us -> 427 us
  local copies, waits for them, and re-layouts: 131 us -> 52.7 us
  Pallas kernels: 303 us -> 317 us
  matrix products: 26.8 us -> 14.5 us
    reshape x14 -> x6, local copies, waits for them, and re-layouts: 103 us -> 43.2 us  [the longest x4 24.9 us: grid(): return received.reshape(tall, cols, depth, rows, width)]
    transpose x4 -> x0, local copies, waits for them, and re-layouts: 27.7 us -> none  [matrices(): grid.transpose(2, 0, 3, 1, 4).reshape(depth, tall * rows, cols * width)]
    pallas_call x0 -> x2, Pallas kernels: none -> 15.1 us  [product(): pl.pallas_call(functools.partial(product_kernel, turned), out_shape=jax.S...]
    dot_general x2 -> x0, matrix products: 12.3 us -> none  [the longest x1 6.45 us: direct_shards(): jnp.einsum('cik,cjk->cij', matrices(left, inner), matrices(right, halves...]
    unnamed x42 -> x50, local copies, waits for them, and re-layouts: 0.11 us -> 9.27 us
where the time goes in v2:
time: 428 us; the launch traced here: 427 us
  Pallas kernels  317 us (74%)
  local copies, waits for them, and re-layouts  52.7 us (12%)
  other arithmetic  41.8 us (10%)
  matrix products  14.5 us (3%)
    pallas_call x4, Pallas kernels, exchange(): pl.pallas_call(functools.partial(exchange_kernel, plan, sizes), out_shape...  302 us
    reshape x4, local copies, waits for them, and re-layouts, grid(): return received.reshape(tall, cols, depth, rows, width)  24.9 us
    reshape x2, local copies, waits for them, and re-layouts, blocks(): return part.reshape(-1, depth, span)  18.4 us
    pallas_call x2, Pallas kernels, product(): pl.pallas_call(functools.partial(product_kernel, turned), out_shape=jax.S...  15.1 us
    reduce_sum x4, other arithmetic, layer_norm(): variance = jnp.mean(centred * centred, axis=reduce_axis, keepdims=True)  9.96 us
    unnamed x50, local copies, waits for them, and re-layouts  9.27 us

profile of v2, /device:TPU:11, one launch (start us, length us, event | category | flops | bytes accessed | tf_op | source)
XLA Modules:
  0.0 426.9 jit_solution(14377882702143243379)
XLA Ops:
  0.0 2.7 convert_reduce_fusion
  2.8 4.4 %multiply_reduce_fusion.3 = f32[96,96]{1,0:T(8,128)S(1)} fusion(bf16[96,96,128]{2,1,0:T(8,128)(2,1)} %param.11, f32[96,96]{1,0:T(8,128)S(1)} %broadcast_multiply_fusion), kind=kLoop, calls=%fused_computation.55 | loop fusion | flops 4709376 | bytes 2433024 | tf_op jit(solution)/shard_map/reduce_sum | solution.py:16
  7.4 4.9 %fusion.32 = bf16[9216,128]{1,0:T(8,128)(2,1)S(1)} fusion(bf16[96,96,128]{2,1,0:T(8,128)(2,1)S(1)} %copy-done.8, f32[128]{0:T(128)S(1)} %copy-done.16, f32[9216]{0:T(1024)S(1)} %rsqrt.36, f32[9216]{0:T(1024)S(1)} %div.45), kind=kLoop, calls=%fused_computation.49 | loop fusion | flops 5898240 | bytes 4792832 | tf_op jit(solution)/shard_map/convert_element_type | solution.py:23
  12.3 2.6 convolution_bitcast_fusion.1
  15.0 3.9 fusion.19
  18.9 111.4 %shard_map.109 = (bf16[8,16,9216]{2,1,0:T(8,128)(2,1)}, bf16[16,16,9216]{2,1,0:T(8,128)(2,1)}) custom-call(bf16[8,16,9216]{2,1,0:T(8,128)(2,1)} %bitcast.49, bf16[8,16,9216]{2,1,0:T(8,128)(2,1)} %bitcast.48), custom_call_target="tpu_custom_call" | custom-call | tf_op jit(solution)/shard_map/pallas_call | solution.py:125
  130.4 10.1 %reshape.109.right_ref = bf16[4,4,16,96,96]{4,3,2,1,0:T(8,128)(2,1)} reshape(bf16[16,16,9216]{2,1,0:T(8,128)(2,1)} %get-tuple-element.10) | data formatting | bytes 9437184 | tf_op jit(solution)/shard_map/reshape | solution.py:211
  140.4 4.5 %reshape.108.left_ref = bf16[2,4,16,96,96]{4,3,2,1,0:T(8,128)(2,1)S(1)} reshape(bf16[8,16,9216]{2,1,0:T(8,128)(2,1)} %get-tuple-element.9) | data formatting | bytes 4718592 | tf_op jit(solution)/shard_map/reshape | solution.py:211
  144.9 2.8 copy-done.2
  147.7 4.9 %shard_map.110 = bf16[2,4,16,96,96]{4,3,2,1,0:T(8,128)(2,1)S(1)} custom-call(bf16[2,4,16,96,96]{4,3,2,1,0:T(8,128)(2,1)S(1)} %reshape.108.left_ref, bf16[4,4,16,96,96]{4,3,2,1,0:T(8,128)(2,1)S(1)} %copy-done.2), custom_call_target="tpu_custom_call" | custom-call | flops 905969664 | bytes 7077888 | tf_op jit(solution)/shard_map/pallas_call | solution.py:173
  152.6 1.7 copy-done.4
  154.3 6.7 %reshape.110.refs_0_ = bf16[8,16,9216]{2,1,0:T(8,128)(2,1)} reshape(bf16[2,4,16,96,96]{4,3,2,1,0:T(8,128)(2,1)} %copy-done.4) | data formatting | bytes 4718592 | tf_op jit(solution)/shard_map/reshape | solution.py:208
  161.0 29.8 %shard_map.111 = bf16[8,16,9216]{2,1,0:T(8,128)(2,1)} custom-call(bf16[8,16,9216]{2,1,0:T(8,128)(2,1)} %reshape.110.refs_0_), custom_call_target="tpu_custom_call" | custom-call | tf_op jit(solution)/shard_map/pallas_call | solution.py:125
  190.9 2.2 convert_reduce_fusion.2
  193.1 2.3 multiply_reduce_fusion.2
  196.2 1.4 fusion.9
  197.9 2.0 fusion.36
  199.9 2.7 multiply_reduce_fusion.1
  202.7 2.8 convolution_bitcast_fusion
  205.6 4.0 fusion.11
  209.6 54.5 %shard_map.112 = (bf16[8,16,9216]{2,1,0:T(8,128)(2,1)}, bf16[8,16,9216]{2,1,0:T(8,128)(2,1)}) custom-call(bf16[8,16,9216]{2,1,0:T(8,128)(2,1)} %bitcast.51, bf16[8,16,9216]{2,1,0:T(8,128)(2,1)} %bitcast.50), custom_call_target="tpu_custom_call" | custom-call | tf_op jit(solution)/shard_map/pallas_call | solution.py:125
  264.1 4.5 %reshape.111.left_ref = bf16[2,4,16,96,96]{4,3,2,1,0:T(8,128)(2,1)S(1)} reshape(bf16[8,16,9216]{2,1,0:T(8,128)(2,1)} %get-tuple-element.11) | data formatting | bytes 4718592 | tf_op jit(solution)/shard_map/reshape | solution.py:211
  268.6 5.9 %reshape.112.right_ref = bf16[2,4,16,96,96]{4,3,2,1,0:T(8,128)(2,1)} reshape(bf16[8,16,9216]{2,1,0:T(8,128)(2,1)} %get-tuple-element.12) | data formatting | bytes 4718592 | tf_op jit(solution)/shard_map/reshape | solution.py:211
  274.5 1.9 copy-done.5
  276.3 10.2 %shard_map.113 = bf16[4,4,16,96,96]{4,3,2,1,0:T(8,128)(2,1)S(1)} custom-call(bf16[2,4,16,96,96]{4,3,2,1,0:T(8,128)(2,1)S(1)} %reshape.111.left_ref, bf16[2,4,16,96,96]{4,3,2,1,0:T(8,128)(2,1)S(1)} %copy-done.5), custom_call_target="tpu_custom_call" | custom-call | flops 905969664 | bytes 4718592 | tf_op jit(solution)/shard_map/pallas_call | solution.py:173
  286.6 2.6 copy-done.3
  289.1 11.7 %reshape.113.refs_0_ = bf16[16,16,9216]{2,1,0:T(8,128)(2,1)} reshape(bf16[4,4,16,96,96]{4,3,2,1,0:T(8,128)(2,1)} %copy-done.3) | data formatting | bytes 9437184 | tf_op jit(solution)/shard_map/reshape | solution.py:208
  300.8 106.5 %shard_map.114 = bf16[16,16,9216]{2,1,0:T(8,128)(2,1)} custom-call(bf16[16,16,9216]{2,1,0:T(8,128)(2,1)} %reshape.113.refs_0_), custom_call_target="tpu_custom_call" | custom-call | tf_op jit(solution)/shard_map/pallas_call | solution.py:125
  407.3 7.3 %convert_element_type.86 = f32[16,16,9216]{2,1,0:T(8,128)} convert(bf16[16,16,9216]{2,1,0:T(8,128)(2,1)} %shard_map.114) | non-fusion elementwise | flops 2359296 | bytes 14155776 | tf_op jit(solution)/shard_map/convert_element_type | solution.py:228
  414.6 5.2 %bitcast_reduce_fusion = f32[128,9216]{1,0:T(8,128)S(1)} fusion(f32[2,128,9216]{2,1,0:T(8,128)} %bitcast.46), kind=kLoop, calls=%fused_computation.17 | loop fusion | flops 1179648 | bytes 14155776 | tf_op jit(solution)/shard_map/reduce_sum | solution.py:228
  421.3 2.7 fusion.10
  424.0 3.0 fusion.7
  (61 shorter events, 2.6 us)
Async XLA Ops:
  0.0 12.3 %copy-start = (bf16[128,512]{1,0:T(8,128)(2,1)S(1)}, bf16[128,512]{1,0:T(8,128)(2,1)}, u32[]{:S(2)}) copy-start(bf16[128,512]{1,0:T(8,128)(2,1)} %param.13) | copy-start | bytes 393220
  0.0 7.3 %copy-start.8 = (bf16[96,96,128]{2,1,0:T(8,128)(2,1)S(1)}, bf16[96,96,128]{2,1,0:T(8,128)(2,1)}, u32[]{:S(2)}) copy-start(bf16[96,96,128]{2,1,0:T(8,128)(2,1)} %param.11) | copy-start | bytes 7077892
  0.0 7.3 %copy-start.16 = (f32[128]{0:T(128)S(1)}, f32[128]{0:T(128)}, u32[]{:S(2)}) copy-start(f32[128]{0:T(128)} %param.12) | copy-start | bytes 1540
  12.3 2.7 copy-start.10
  144.9 2.8 copy-start.2
  152.6 1.7 copy-start.4
  161.0 34.5 %copy-start.17 = (f32[128]{0:T(128)S(1)}, f32[128]{0:T(128)}, u32[]{:S(2)}) copy-start(f32[128]{0:T(128)} %param.15) | copy-start | bytes 1540
  190.8 4.6 %copy-start.7 = (bf16[8,16,9216]{2,1,0:T(8,128)(2,1)S(1)}, bf16[8,16,9216]{2,1,0:T(8,128)(2,1)}, u32[]{:S(2)}) copy-start(bf16[8,16,9216]{2,1,0:T(8,128)(2,1)} %shard_map.111) | copy-start | bytes 7077892
  190.9 5.3 %copy-start.11 = (bf16[9216,128]{1,0:T(8,128)(2,1)S(1)}, bf16[9216,128]{1,0:T(8,128)(2,1)}, u32[]{:S(2)}) copy-start(bf16[9216,128]{1,0:T(8,128)(2,1)} %copy-done.10) | copy-start | bytes 7077892
  190.9 5.3 %copy-start.19 = (bf16[128,128]{1,0:T(8,128)(2,1)S(1)}, bf16[128,128]{1,0:T(8,128)(2,1)}, u32[]{:S(2)}) copy-start(bf16[128,128]{1,0:T(8,128)(2,1)} %param.14) | copy-start | bytes 98308
  196.2 1.7 copy-start.9
  196.2 1.7 copy-start.13
  199.9 5.7 %copy-start.6 = (f32[9216,128]{1,0:T(8,128)}, f32[9216,128]{1,0:T(8,128)S(1)}, u32[]{:S(2)}) copy-start(f32[9216,128]{1,0:T(8,128)S(1)} %get-tuple-element.18) | copy-start | bytes 14155780
  199.9 2.8 copy-start.12
  199.9 2.8 copy-start.15
  274.5 1.9 copy-start.5
  286.6 2.6 copy-start.3
  407.3 12.5 %slice-start.2 = ((s8[4718592]{0:T(1024)(128)(4,1)}), s8[4194304]{0:T(1024)(128)(4,1)S(1)}, s32[]{:S(2)}) async-start(s8[4718592]{0:T(1024)(128)(4,1)} %bitcast.44), calls=%async_computation.2 | async-start | bytes 8388608
  414.6 5.2 %slice-start.3 = ((s8[4718592]{0:T(1024)(128)(4,1)}), s8[524288]{0:T(1024)(128)(4,1)S(1)}, s32[]{:S(2)}) async-start(s8[4718592]{0:T(1024)(128)(4,1)} %bitcast.44), calls=%async_computation.3 | async-start | bytes 1048576
  414.6 6.6 %slice-start = ((s8[4718592]{0:T(1024)(128)(4,1)}), s8[4194304]{0:T(1024)(128)(4,1)S(1)}, s32[]{:S(2)}) async-start(s8[4718592]{0:T(1024)(128)(4,1)} %bitcast.42), calls=%async_computation | async-start | bytes 8388608
  414.6 6.6 %slice-start.1 = ((s8[4718592]{0:T(1024)(128)(4,1)}), s8[524288]{0:T(1024)(128)(4,1)S(1)}, s32[]{:S(2)}) async-start(s8[4718592]{0:T(1024)(128)(4,1)} %bitcast.42), calls=%async_computation.1 | async-start | bytes 1048576
  419.8 1.4 copy-start.20
  421.2 2.7 copy-start.14
  421.2 2.7 copy-start.18
  421.2 5.7 %copy-start.1 = (bf16[128,512]{1,0:T(8,128)(2,1)S(1)}, bf16[128,512]{1,0:T(8,128)(2,1)}, u32[]{:S(2)}) copy-start(bf16[128,512]{1,0:T(8,128)(2,1)} %param.13) | copy-start | bytes 393220

commit v3 on v2

--- a/solution.py
+++ b/solution.py
@@ -39,13 +39,16 @@
     return result.astype(jnp.bfloat16).reshape(pair_state.shape)
 
 
-def exchange_kernel(plan, sizes, *refs):
+def exchange_kernel(plan, sizes, opened, *refs):
     halves, inner, chans, subs = sizes
     cols = chans * subs
     block = inner * cols
     count = len(plan)
     sources, targets = refs[:count], refs[count : 2 * count]
     sems = refs[2 * count : 5 * count]
+    opens = targets
+    if opened:
+        targets = refs[5 * count : 6 * count]
     row = lax.axis_index("dap")
     col = lax.axis_index("chan") * subs + lax.axis_index("sub")
     mine = lax.rem(row, inner) * cols + col
@@ -93,6 +96,9 @@
                 device_id_type=pl.DeviceIdType.MESH,
             )
             copy.start()
+            if opened:
+                started.append((copy, copy))
+                continue
             arriving = pltpu.make_async_remote_copy(
                 src_ref=piece,
                 dst_ref=target.at[back],
@@ -102,33 +108,75 @@
                 device_id_type=pl.DeviceIdType.MESH,
             )
             started.append((copy, arriving))
+    if not opened:
+        for copy, arriving in started:
+            if arriving is None:
+                copy.wait()
+            else:
+                copy.wait_send()
+                arriving.wait_recv()
+        return
+
+    def unfold(target, open_ref, slot):
+        rows, width = open_ref.shape[2:]
+        open_ref[slot] = target[slot].reshape(target.shape[1], rows, width)
+
+    for (varies, spans), source, target, open_ref, (sent, got, kept) in zip(
+        plan, sources, targets, opens, [sems[3 * n : 3 * n + 3] for n in range(count)]
+    ):
+        slots = whole if spans else block
+        base = me if spans else mine
+        pltpu.make_async_copy(source.at[me if varies else mine], target.at[base], kept).wait()
+        unfold(target, open_ref, base)
+
+        def arrive(off, carry, slots=slots, base=base, source=source, target=target,
+                   open_ref=open_ref, sent=sent, got=got):
+            back = lax.rem(base - off + slots, slots)
+            arriving = pltpu.make_async_remote_copy(
+                src_ref=source.at[0],
+                dst_ref=target.at[back],
+                send_sem=sent.at[off],
+                recv_sem=got.at[off],
+                device_id=place(back if slots == whole else half * block + back),
+                device_id_type=pl.DeviceIdType.MESH,
+            )
+            arriving.wait_recv()
+            unfold(target, open_ref, back)
+            return carry
+
+        lax.fori_loop(1, slots, arrive, 0)
     for copy, arriving in started:
-        if arriving is None:
-            copy.wait()
-        else:
+        if arriving is not None:
             copy.wait_send()
-            arriving.wait_recv()
-
-
-def exchange(plan, sizes, number, *arrays):
+
+
+def exchange(plan, sizes, number, *arrays, opened=None):
     halves, inner, chans, subs = sizes
     block = inner * chans * subs
-    shapes, sems = [], []
+    shapes, sems, landing = [], [], []
     for (varies, spans), array in zip(plan, arrays):
         slots = halves * block if spans else block
-        shapes.append(jax.ShapeDtypeStruct((slots,) + array.shape[1:], array.dtype))
+        if opened:
+            shapes.append(jax.ShapeDtypeStruct((slots, array.shape[1]) + opened, array.dtype))
+            landing.append(pltpu.VMEM((slots,) + array.shape[1:], array.dtype))
+        else:
+            shapes.append(jax.ShapeDtypeStruct((slots,) + array.shape[1:], array.dtype))
         sems += [
             pltpu.SemaphoreType.DMA((slots,)),
             pltpu.SemaphoreType.DMA((slots,)),
             pltpu.SemaphoreType.DMA,
         ]
     return pl.pallas_call(
-        functools.partial(exchange_kernel, plan, sizes),
+        functools.partial(exchange_kernel, plan, sizes, opened is not None),
         out_shape=shapes,
         in_specs=[pl.BlockSpec(memory_space=pl.ANY)] * len(arrays),
-        out_specs=[pl.BlockSpec(memory_space=pl.ANY)] * len(arrays),
-        scratch_shapes=sems,
-        compiler_params=pltpu.CompilerParams(collective_id=number, has_side_effects=True),
+        out_specs=[pl.BlockSpec(memory_space=pltpu.VMEM if opened else pl.ANY)] * len(arrays),
+        scratch_shapes=sems + landing,
+        compiler_params=pltpu.CompilerParams(
+            collective_id=number,
+            has_side_effects=True,
+            vmem_limit_bytes=40 * 2**20 if opened else None,
+        ),
     )(*arrays)
 
 
@@ -212,7 +260,8 @@
 
     left, right, gating = project_in(pair_input, first_gain, first_project, first_gate)
     left, right = exchange(
-        ((False, False), (False, True)), sizes, 0, blocks(left), blocks(right)
+        ((False, False), (False, True)), sizes, 0, blocks(left), blocks(right),
+        opened=(rows, width),
     )
     mixture = product(False, grid(left, inner), grid(right, halves * inner))
     (mixture,) = exchange(((False, False),), sizes, 1, blocks(mixture))
@@ -221,11 +270,13 @@
     )
     left, right, gating = project_in(middle, second_gain, second_project, second_gate)
     left, right = exchange(
-        ((False, False), (False, False)), sizes, 2, blocks(left), blocks(right)
+        ((False, False), (False, False)), sizes, 2, blocks(left), blocks(right),
+        opened=(rows, width),
     )
     mixture = product(True, grid(left, inner), grid(right, inner))
     (mixture,) = exchange(((True, True),), sizes, 3, blocks(mixture))
-    mixture = mixture.reshape(halves, features, span).astype(jnp.float32).sum(axis=0)
+    mixture = mixture.reshape(halves, features, span)
+    mixture = sum(mixture[n].astype(jnp.float32) for n in range(halves))
     return finish(middle, mixture, gating, second_norm, second_final)
 
 

time: 428 us -> 408 us (0.953)
  local copies, waits for them, and re-layouts: 52.7 us -> 20.7 us
  matrix products: 14.5 us -> 25.9 us
    reshape x4 -> x0, local copies, waits for them, and re-layouts: 24.9 us -> none  [grid(): return received.reshape(tall, cols, depth, rows, width)]
    dot_general x2, matrix products: 5.49 us -> 17.6 us  [project_in(): jnp.einsum('xc,cd->dx', normed, project, preferred_element_type=jnp.float32)]
    convert_element_type x2, other arithmetic: 7.93 us -> 15.4 us  [project_in(): right_part.astype(jnp.bfloat16).reshape(features, row_count, col_count)]
    convert_element_type x1 -> x0, other arithmetic: 7.27 us -> none  [direct_shards(): mixture.reshape(halves, features, span).astype(jnp.float32).sum(axis=0)]
    unnamed x50 -> x42, local copies, waits for them, and re-layouts: 9.27 us -> 3.71 us
    reduce_sum x1 -> x0, other arithmetic: 5.2 us -> none  [direct_shards(): mixture.reshape(halves, features, span).astype(jnp.float32).sum(axis=0)]
where the time goes in v3:
time: 408 us
  Pallas kernels  320 us (78%)
  other arithmetic  40.4 us (10%)
  matrix products  25.9 us (6%)
  local copies, waits for them, and re-layouts  20.7 us (5%)
    pallas_call x4, Pallas kernels, exchange(): pl.pallas_call(functools.partial(exchange_kernel, plan, sizes, opened is...  305 us
    dot_general x2, matrix products, project_in(): jnp.einsum('xc,cd->dx', normed, project, preferred_element_type=jnp.float32)  17.6 us
    reshape x2, local copies, waits for them, and re-layouts, blocks(): return part.reshape(-1, depth, span)  16.8 us
    convert_element_type x2, other arithmetic, project_in(): right_part.astype(jnp.bfloat16).reshape(features, row_count, col_count)  15.4 us
    pallas_call x2, Pallas kernels, product(): pl.pallas_call(functools.partial(product_kernel, turned), out_shape=jax.S...  15.3 us
    reduce_sum x4, other arithmetic, layer_norm(): variance = jnp.mean(centred * centred, axis=reduce_axis, keepdims=True)  10.4 us

profile of v3, /device:TPU:11, one launch (start us, length us, event | category | flops | bytes accessed | tf_op | source)
XLA Modules:
  0.0 407.6 jit_solution(1640254651797746063)
XLA Ops:
  0.0 2.7 convert_reduce_fusion
  2.8 4.4 %multiply_reduce_fusion.3 = f32[96,96]{1,0:T(8,128)S(1)} fusion(bf16[96,96,128]{2,1,0:T(8,128)(2,1)} %param.11, f32[96,96]{1,0:T(8,128)S(1)} %broadcast_multiply_fusion), kind=kLoop, calls=%fused_computation.58 | loop fusion | flops 4709376 | bytes 2433024 | tf_op jit(solution)/shard_map/reduce_sum | solution.py:16
  7.1 0.1 rsqrt.36
  7.2 0.1 div.45
  7.4 4.9 %fusion.35 = bf16[9216,128]{1,0:T(8,128)(2,1)S(1)} fusion(bf16[96,96,128]{2,1,0:T(8,128)(2,1)S(1)} %copy-done.6, f32[128]{0:T(128)S(1)} %copy-done.14, f32[9216]{0:T(1024)S(1)} %rsqrt.36, f32[9216]{0:T(1024)S(1)} %div.45), kind=kLoop, calls=%fused_computation.52 | loop fusion | flops 5898240 | bytes 4792832 | tf_op jit(solution)/shard_map/convert_element_type | solution.py:23
  12.3 7.9 %convolution_bitcast_fusion.1 = f32[512,9216]{1,0:T(8,128)} fusion(bf16[9216,128]{1,0:T(8,128)(2,1)S(1)} %fusion.35, bf16[128,512]{1,0:T(8,128)(2,1)S(1)} %copy-done), kind=kOutput, calls=%fused_computation.1 | convolution fusion | flops 1207959552 | bytes 21364736 | tf_op jit(solution)/shard_map/xc,cd->dx/dot_general | solution.py:24
  20.2 7.7 %fusion.19 = (bf16[128,9216]{1,0:T(8,128)(2,1)S(1)}, bf16[128,9216]{1,0:T(8,128)(2,1)S(1)}) fusion(f32[512,9216]{1,0:T(8,128)} %convolution_bitcast_fusion.1), kind=kLoop, calls=%fused_computation.30 | loop fusion | flops 11796480 | bytes 23592960 | tf_op jit(solution)/shard_map/convert_element_type | solution.py:28
  27.9 111.4 %shard_map.109 = (bf16[8,16,96,96]{3,2,1,0:T(8,128)(2,1)S(1)}, bf16[16,16,96,96]{3,2,1,0:T(8,128)(2,1)S(1)}) custom-call(bf16[8,16,9216]{2,1,0:T(8,128)(2,1)S(1)} %bitcast.53, bf16[8,16,9216]{2,1,0:T(8,128)(2,1)S(1)} %bitcast.52), custom_call_target="tpu_custom_call" | custom-call | tf_op jit(solution)/shard_map/pallas_call | solution.py:169
  139.4 4.9 %shard_map.110 = bf16[2,4,16,96,96]{4,3,2,1,0:T(8,128)(2,1)S(1)} custom-call(bf16[2,4,16,96,96]{4,3,2,1,0:T(8,128)(2,1)S(1)} %bitcast.57, bf16[4,4,16,96,96]{4,3,2,1,0:T(8,128)(2,1)S(1)} %bitcast.56), custom_call_target="tpu_custom_call" | custom-call | flops 905969664 | bytes 7077888 | tf_op jit(solution)/shard_map/pallas_call | solution.py:221
  144.3 5.1 %reshape.120.refs_0_ = bf16[8,16,9216]{2,1,0:T(8,128)(2,1)} reshape(bf16[2,4,16,96,96]{4,3,2,1,0:T(8,128)(2,1)S(1)} %shard_map.110) | data formatting | bytes 4718592 | tf_op jit(solution)/shard_map/reshape | solution.py:256
  149.4 29.9 %shard_map.111 = bf16[8,16,9216]{2,1,0:T(8,128)(2,1)} custom-call(bf16[8,16,9216]{2,1,0:T(8,128)(2,1)} %reshape.120.refs_0_), custom_call_target="tpu_custom_call" | custom-call | tf_op jit(solution)/shard_map/pallas_call | solution.py:169
  179.3 2.2 convert_reduce_fusion.1
  181.5 2.3 multiply_reduce_fusion.2
  183.9 0.7 fusion.32
  184.7 1.4 fusion.9
  186.1 0.2 copy-done.7
  186.3 2.0 fusion.37
  188.4 2.7 multiply_reduce_fusion.1
  191.1 9.7 %convolution_bitcast_fusion = f32[512,9216]{1,0:T(8,128)} fusion(bf16[128,512]{1,0:T(8,128)(2,1)S(1)} %copy-done.10, f32[9216,128]{1,0:T(8,128)S(1)} %get-tuple-element.20, f32[128]{0:T(128)S(1)} %copy-done.13, f32[9216]{0:T(1024)S(1)} %add_rsqrt_fusion.2, f32[9216]{0:T(1024)S(1)} %broadcast_multiply_fusion.2), kind=kOutput, calls=%fused_computation | convolution fusion | flops 1212678144 | bytes 23798272 | tf_op jit(solution)/shard_map/xc,cd->dx/dot_general | solution.py:24
  200.8 7.7 %fusion.11 = (bf16[128,9216]{1,0:T(8,128)(2,1)S(1)}, bf16[128,9216]{1,0:T(8,128)(2,1)S(1)}) fusion(f32[512,9216]{1,0:T(8,128)} %convolution_bitcast_fusion), kind=kLoop, calls=%fused_computation.18 | loop fusion | flops 11796480 | bytes 23592960 | tf_op jit(solution)/shard_map/convert_element_type | solution.py:28
  208.5 54.8 %shard_map.112 = (bf16[8,16,96,96]{3,2,1,0:T(8,128)(2,1)S(1)}, bf16[8,16,96,96]{3,2,1,0:T(8,128)(2,1)S(1)}) custom-call(bf16[8,16,9216]{2,1,0:T(8,128)(2,1)S(1)} %bitcast.55, bf16[8,16,9216]{2,1,0:T(8,128)(2,1)S(1)} %bitcast.54), custom_call_target="tpu_custom_call" | custom-call | tf_op jit(solution)/shard_map/pallas_call | solution.py:169
  263.3 10.4 %shard_map.113 = bf16[4,4,16,96,96]{4,3,2,1,0:T(8,128)(2,1)S(1)} custom-call(bf16[2,4,16,96,96]{4,3,2,1,0:T(8,128)(2,1)S(1)} %bitcast.58, bf16[2,4,16,96,96]{4,3,2,1,0:T(8,128)(2,1)S(1)} %bitcast.59), custom_call_target="tpu_custom_call" | custom-call | flops 905969664 | bytes 4718592 | tf_op jit(solution)/shard_map/pallas_call | solution.py:221
  273.8 2.6 copy-done.2
  276.4 11.7 %reshape.123.refs_0_ = bf16[16,16,9216]{2,1,0:T(8,128)(2,1)} reshape(bf16[4,4,16,96,96]{4,3,2,1,0:T(8,128)(2,1)} %copy-done.2) | data formatting | bytes 9437184 | tf_op jit(solution)/shard_map/reshape | solution.py:256
  288.1 108.8 %shard_map.114 = bf16[16,16,9216]{2,1,0:T(8,128)(2,1)} custom-call(bf16[16,16,9216]{2,1,0:T(8,128)(2,1)} %reshape.123.refs_0_), custom_call_target="tpu_custom_call" | custom-call | tf_op jit(solution)/shard_map/pallas_call | solution.py:169
  396.9 3.2 fusion.36
  400.1 0.5 copy-done.4
  400.7 1.0 multiply_reduce_fusion
  401.7 0.7 fusion.29
  402.5 0.2 copy-done.18
  402.7 2.7 fusion.10
  405.3 2.3 fusion.7
  (47 shorter events, 0.2 us)
Async XLA Ops:
  0.0 12.3 %copy-start = (bf16[128,512]{1,0:T(8,128)(2,1)S(1)}, bf16[128,512]{1,0:T(8,128)(2,1)}, u32[]{:S(2)}) copy-start(bf16[128,512]{1,0:T(8,128)(2,1)} %param.13) | copy-start | bytes 393220
  0.0 7.3 %copy-start.6 = (bf16[96,96,128]{2,1,0:T(8,128)(2,1)S(1)}, bf16[96,96,128]{2,1,0:T(8,128)(2,1)}, u32[]{:S(2)}) copy-start(bf16[96,96,128]{2,1,0:T(8,128)(2,1)} %param.11) | copy-start | bytes 7077892
  0.0 7.3 %copy-start.14 = (f32[128]{0:T(128)S(1)}, f32[128]{0:T(128)}, u32[]{:S(2)}) copy-start(f32[128]{0:T(128)} %param.12) | copy-start | bytes 1540
  12.3 7.9 %copy-start.8 = (bf16[9216,128]{1,0:T(8,128)(2,1)}, bf16[9216,128]{1,0:T(8,128)(2,1)S(1)}, u32[]{:S(2)}) copy-start(bf16[9216,128]{1,0:T(8,128)(2,1)S(1)} %fusion.35) | copy-start | bytes 7077892
  149.4 34.5 %copy-start.15 = (f32[128]{0:T(128)S(1)}, f32[128]{0:T(128)}, u32[]{:S(2)}) copy-start(f32[128]{0:T(128)} %param.15) | copy-start | bytes 1540
  179.3 4.6 %copy-start.5 = (bf16[8,16,9216]{2,1,0:T(8,128)(2,1)S(1)}, bf16[8,16,9216]{2,1,0:T(8,128)(2,1)}, u32[]{:S(2)}) copy-start(bf16[8,16,9216]{2,1,0:T(8,128)(2,1)} %shard_map.111) | copy-start | bytes 7077892
  179.3 5.3 %copy-start.9 = (bf16[9216,128]{1,0:T(8,128)(2,1)S(1)}, bf16[9216,128]{1,0:T(8,128)(2,1)}, u32[]{:S(2)}) copy-start(bf16[9216,128]{1,0:T(8,128)(2,1)} %copy-done.8) | copy-start | bytes 7077892
  179.3 5.3 %copy-start.17 = (bf16[128,128]{1,0:T(8,128)(2,1)S(1)}, bf16[128,128]{1,0:T(8,128)(2,1)}, u32[]{:S(2)}) copy-start(bf16[128,128]{1,0:T(8,128)(2,1)} %param.14) | copy-start | bytes 98308
  184.6 1.7 copy-start.7
  184.6 1.7 copy-start.11
  188.3 12.5 %copy-start.3 = (f32[9216,128]{1,0:T(8,128)}, f32[9216,128]{1,0:T(8,128)S(1)}, u32[]{:S(2)}) copy-start(f32[9216,128]{1,0:T(8,128)S(1)} %get-tuple-element.20) | copy-start | bytes 14155780
  188.3 2.8 copy-start.10
  188.3 2.8 copy-start.13
  273.7 2.6 copy-start.2
  396.9 3.8 copy-start.4
  400.1 2.3 slice-start
  400.7 1.0 copy-start.16
  400.7 1.8 slice-start.1
  401.7 1.0 copy-start.18
  402.6 2.7 copy-start.12
  402.6 5.0 %copy-start.1 = (bf16[128,512]{1,0:T(8,128)(2,1)S(1)}, bf16[128,512]{1,0:T(8,128)(2,1)}, u32[]{:S(2)}) copy-start(bf16[128,512]{1,0:T(8,128)(2,1)} %param.13) | copy-start | bytes 393220

commit v4 on v3

--- a/solution.py
+++ b/solution.py
@@ -150,6 +150,84 @@
             copy.wait_send()
 
 
+def fold_kernel(spans, sizes, source, target, sent, got, kept, flat):
+    halves, inner, chans, subs = sizes
+    cols = chans * subs
+    block = inner * cols
+    slots = halves * block if spans else block
+    row = lax.axis_index("dap")
+    col = lax.axis_index("chan") * subs + lax.axis_index("sub")
+    first = 0 if spans else (row // inner) * block
+    base = row * cols + col - first
+
+    def place(q):
+        owner_row, owner_col = (first + q) // cols, lax.rem(q, cols)
+        return {"dap": owner_row, "chan": owner_col // subs, "sub": lax.rem(owner_col, subs)}
+
+    def push(off, slot):
+        q = lax.rem(base + off, slots)
+        return pltpu.make_async_remote_copy(
+            src_ref=flat.at[q],
+            dst_ref=target.at[slot],
+            send_sem=sent.at[off],
+            recv_sem=got.at[off],
+            device_id=place(q),
+            device_id_type=pl.DeviceIdType.MESH,
+        )
+
+    def fold(q):
+        flat[q] = source[q].reshape(flat.shape[1:])
+
+    barrier = pltpu.get_barrier_semaphore()
+    for off in range(1, slots):
+        pl.semaphore_signal(
+            barrier,
+            inc=1,
+            device_id=place(lax.rem(base + off, slots)),
+            device_id_type=pl.DeviceIdType.MESH,
+        )
+    pl.semaphore_wait(barrier, slots - 1)
+
+    def send(off, carry):
+        fold(lax.rem(base + off, slots))
+        push(off, base).start()
+        return carry
+
+    lax.fori_loop(1, slots, send, 0)
+    fold(base)
+    own = pltpu.make_async_copy(flat.at[base], target.at[base], kept)
+    own.start()
+
+    def finish_off(off, carry):
+        copy = push(off, lax.rem(base - off + slots, slots))
+        copy.wait_send()
+        copy.wait_recv()
+        return carry
+
+    lax.fori_loop(1, slots, finish_off, 0)
+    own.wait()
+
+
+def fold_exchange(spans, sizes, number, array):
+    slots, depth, rows, width = array.shape
+    flat = (slots, depth, rows * width)
+    return pl.pallas_call(
+        functools.partial(fold_kernel, spans, sizes),
+        out_shape=jax.ShapeDtypeStruct(flat, array.dtype),
+        in_specs=[pl.BlockSpec(memory_space=pltpu.VMEM)],
+        out_specs=pl.BlockSpec(memory_space=pl.ANY),
+        scratch_shapes=[
+            pltpu.SemaphoreType.DMA((slots,)),
+            pltpu.SemaphoreType.DMA((slots,)),
+            pltpu.SemaphoreType.DMA,
+            pltpu.VMEM(flat, array.dtype),
+        ],
+        compiler_params=pltpu.CompilerParams(
+            collective_id=number, has_side_effects=True, vmem_limit_bytes=24 * 2**20
+        ),
+    )(array)
+
+
 def exchange(plan, sizes, number, *arrays, opened=None):
     halves, inner, chans, subs = sizes
     block = inner * chans * subs
@@ -175,7 +253,7 @@
         compiler_params=pltpu.CompilerParams(
             collective_id=number,
             has_side_effects=True,
-            vmem_limit_bytes=40 * 2**20 if opened else None,
+            vmem_limit_bytes=24 * 2**20 if opened else None,
         ),
     )(*arrays)
 
@@ -224,7 +302,7 @@
         grid=(depth // step,),
         in_specs=[spec(left_tall), spec(right_tall)],
         out_specs=spec(tall),
-        compiler_params=pltpu.CompilerParams(vmem_limit_bytes=40 * 2**20),
+        compiler_params=pltpu.CompilerParams(vmem_limit_bytes=24 * 2**20),
         cost_estimate=pl.CostEstimate(
             flops=flops, bytes_accessed=2 * (left.size + right.size), transcendentals=0
         ),
@@ -264,7 +342,7 @@
         opened=(rows, width),
     )
     mixture = product(False, grid(left, inner), grid(right, halves * inner))
-    (mixture,) = exchange(((False, False),), sizes, 1, blocks(mixture))
+    mixture = fold_exchange(False, sizes, 1, mixture.reshape(-1, depth, rows, width))
     middle = finish(
         pair_input, mixture.reshape(features, span), gating, first_norm, first_final
     )
@@ -274,7 +352,7 @@
         opened=(rows, width),
     )
     mixture = product(True, grid(left, inner), grid(right, inner))
-    (mixture,) = exchange(((True, True),), sizes, 3, blocks(mixture))
+    mixture = fold_exchange(True, sizes, 3, mixture.reshape(-1, depth, rows, width))
     mixture = mixture.reshape(halves, features, span)
     mixture = sum(mixture[n].astype(jnp.float32) for n in range(halves))
     return finish(middle, mixture, gating, second_norm, second_final)

time: 408 us -> 361 us (0.88)
  local copies, waits for them, and re-layouts: 20.7 us -> 1.09 us
  other arithmetic: 40.4 us -> 24 us
  matrix products: 25.9 us -> 14 us
    pallas_call x0 -> x2, Pallas kernels: none -> 140 us  [fold_exchange(): pl.pallas_call(functools.partial(fold_kernel, spans, sizes), out_shape=ja...]
    pallas_call x4 -> x2, Pallas kernels: 305 us -> 166 us  [exchange(): pl.pallas_call(functools.partial(exchange_kernel, plan, sizes, opened is...]
    reshape x2 -> x0, local copies, waits for them, and re-layouts: 16.8 us -> none  [blocks(): return part.reshape(-1, depth, span)]
    dot_general x2, matrix products: 17.6 us -> 5.49 us  [project_in(): jnp.einsum('xc,cd->dx', normed, project, preferred_element_type=jnp.float32)]
    convert_element_type x2, other arithmetic: 15.4 us -> 5 us  [project_in(): right_part.astype(jnp.bfloat16).reshape(features, row_count, col_count)]
    reduce_sum x3, other arithmetic: 8.14 us -> 3.79 us  [layer_norm(): average = jnp.mean(values, axis=reduce_axis, keepdims=True)]
where the time goes in v4:
time: 361 us
  Pallas kernels  321 us (89%)
  other arithmetic  24 us (7%)
  matrix products  14 us (4%)
    pallas_call x2, Pallas kernels, exchange(): pl.pallas_call(functools.partial(exchange_kernel, plan, sizes, opened is...  166 us
    pallas_call x2, Pallas kernels, fold_exchange(): pl.pallas_call(functools.partial(fold_kernel, spans, sizes), out_shape=ja...  140 us
    pallas_call x2, Pallas kernels, product(): pl.pallas_call(functools.partial(product_kernel, turned), out_shape=jax.S...  15.3 us
    reduce_sum x4, other arithmetic, layer_norm(): variance = jnp.mean(centred * centred, axis=reduce_axis, keepdims=True)  8.75 us

profile of v4, /device:TPU:11, one launch (start us, length us, event | category | flops | bytes accessed | tf_op | source)
XLA Modules:
  0.0 360.6 jit_solution(6737907368668605041)
XLA Ops:
  0.0 2.7 convert_reduce_fusion
  2.8 4.4 %multiply_reduce_fusion.3 = f32[96,96]{1,0:T(8,128)S(1)} fusion(bf16[96,96,128]{2,1,0:T(8,128)(2,1)} %param.11, f32[96,96]{1,0:T(8,128)S(1)} %broadcast_multiply_fusion), kind=kLoop, calls=%fused_computation.58 | loop fusion | flops 4709376 | bytes 2433024 | tf_op jit(solution)/shard_map/reduce_sum | solution.py:16
  7.1 0.1 rsqrt.36
  7.2 0.1 div.45
  7.4 4.9 %fusion.35 = bf16[9216,128]{1,0:T(8,128)(2,1)S(1)} fusion(bf16[96,96,128]{2,1,0:T(8,128)(2,1)S(1)} %copy-done.3, f32[128]{0:T(128)S(1)} %copy-done.11, f32[9216]{0:T(1024)S(1)} %rsqrt.36, f32[9216]{0:T(1024)S(1)} %div.45), kind=kLoop, calls=%fused_computation.52 | loop fusion | flops 5898240 | bytes 4792832 | tf_op jit(solution)/shard_map/convert_element_type | solution.py:23
  12.3 2.6 convolution_bitcast_fusion.1
  15.0 2.5 fusion.19
  17.5 111.4 %shard_map.109 = (bf16[8,16,96,96]{3,2,1,0:T(8,128)(2,1)S(1)}, bf16[16,16,96,96]{3,2,1,0:T(8,128)(2,1)S(1)}) custom-call(bf16[8,16,9216]{2,1,0:T(8,128)(2,1)S(1)} %bitcast.53, bf16[8,16,9216]{2,1,0:T(8,128)(2,1)S(1)} %bitcast.52), custom_call_target="tpu_custom_call" | custom-call | tf_op jit(solution)/shard_map/pallas_call | solution.py:247
  128.9 4.9 %shard_map.110 = bf16[2,4,16,96,96]{4,3,2,1,0:T(8,128)(2,1)S(1)} custom-call(bf16[2,4,16,96,96]{4,3,2,1,0:T(8,128)(2,1)S(1)} %bitcast.57, bf16[4,4,16,96,96]{4,3,2,1,0:T(8,128)(2,1)S(1)} %bitcast.56), custom_call_target="tpu_custom_call" | custom-call | flops 905969664 | bytes 7077888 | tf_op jit(solution)/shard_map/pallas_call | solution.py:299
  133.9 30.2 %shard_map.111 = bf16[8,16,9216]{2,1,0:T(8,128)(2,1)S(1)} custom-call(bf16[8,16,96,96]{3,2,1,0:T(8,128)(2,1)S(1)} %bitcast.51), custom_call_target="tpu_custom_call" | custom-call | tf_op jit(solution)/shard_map/pallas_call | solution.py:214
  164.1 0.0 copy-start.6
  164.1 0.4 convert_reduce_fusion.1
  164.5 0.7 multiply_reduce_fusion.2
  165.2 0.7 fusion.32
  166.0 0.0 copy-start.8
  166.0 1.4 fusion.9
  167.4 0.2 copy-done.4
  167.7 2.0 fusion.37
  169.7 2.7 multiply_reduce_fusion.1
  172.5 2.8 convolution_bitcast_fusion
  175.3 2.5 fusion.11
  177.9 54.8 %shard_map.112 = (bf16[8,16,96,96]{3,2,1,0:T(8,128)(2,1)S(1)}, bf16[8,16,96,96]{3,2,1,0:T(8,128)(2,1)S(1)}) custom-call(bf16[8,16,9216]{2,1,0:T(8,128)(2,1)S(1)} %bitcast.55, bf16[8,16,9216]{2,1,0:T(8,128)(2,1)S(1)} %bitcast.54), custom_call_target="tpu_custom_call" | custom-call | tf_op jit(solution)/shard_map/pallas_call | solution.py:247
  232.6 10.4 %shard_map.113 = bf16[4,4,16,96,96]{4,3,2,1,0:T(8,128)(2,1)S(1)} custom-call(bf16[2,4,16,96,96]{4,3,2,1,0:T(8,128)(2,1)S(1)} %bitcast.58, bf16[2,4,16,96,96]{4,3,2,1,0:T(8,128)(2,1)S(1)} %bitcast.59), custom_call_target="tpu_custom_call" | custom-call | flops 905969664 | bytes 4718592 | tf_op jit(solution)/shard_map/pallas_call | solution.py:299
  243.1 109.4 %shard_map.114 = bf16[16,16,9216]{2,1,0:T(8,128)(2,1)S(1)} custom-call(bf16[16,16,96,96]{3,2,1,0:T(8,128)(2,1)S(1)} %bitcast.50), custom_call_target="tpu_custom_call" | custom-call | tf_op jit(solution)/shard_map/pallas_call | solution.py:214
  352.5 0.7 fusion.36
  353.2 1.0 multiply_reduce_fusion
  354.2 0.7 fusion.29
  354.9 0.4 slice-done
  355.3 0.1 slice-done.1
  355.5 0.1 copy-done.15
  355.5 2.7 fusion.10
  358.2 2.4 fusion.7
  (39 shorter events, 0.2 us)
Async XLA Ops:
  0.0 12.3 %copy-start = (bf16[128,512]{1,0:T(8,128)(2,1)S(1)}, bf16[128,512]{1,0:T(8,128)(2,1)}, u32[]{:S(2)}) copy-start(bf16[128,512]{1,0:T(8,128)(2,1)} %param.13) | copy-start | bytes 393220
  0.0 7.3 %copy-start.3 = (bf16[96,96,128]{2,1,0:T(8,128)(2,1)S(1)}, bf16[96,96,128]{2,1,0:T(8,128)(2,1)}, u32[]{:S(2)}) copy-start(bf16[96,96,128]{2,1,0:T(8,128)(2,1)} %param.11) | copy-start | bytes 7077892
  0.0 7.3 %copy-start.11 = (f32[128]{0:T(128)S(1)}, f32[128]{0:T(128)}, u32[]{:S(2)}) copy-start(f32[128]{0:T(128)} %param.12) | copy-start | bytes 1540
  12.3 2.7 copy-start.5
  133.8 31.4 %copy-start.12 = (f32[128]{0:T(128)S(1)}, f32[128]{0:T(128)}, u32[]{:S(2)}) copy-start(f32[128]{0:T(128)} %param.15) | copy-start | bytes 1540
  164.1 1.9 copy-start.6
  164.1 1.9 copy-start.14
  166.0 1.7 copy-start.4
  166.0 1.7 copy-start.8
  169.7 5.7 %copy-start.2 = (f32[9216,128]{1,0:T(8,128)}, f32[9216,128]{1,0:T(8,128)S(1)}, u32[]{:S(2)}) copy-start(f32[9216,128]{1,0:T(8,128)S(1)} %get-tuple-element.20) | copy-start | bytes 14155780
  169.7 2.8 copy-start.7
  169.7 2.8 copy-start.10
  353.1 2.2 slice-start
  353.2 1.1 copy-start.13
  353.2 2.3 slice-start.1
  354.2 1.3 copy-start.15
  355.5 2.7 copy-start.9
  355.5 5.1 %copy-start.1 = (bf16[128,512]{1,0:T(8,128)(2,1)S(1)}, bf16[128,512]{1,0:T(8,128)(2,1)}, u32[]{:S(2)}) copy-start(bf16[128,512]{1,0:T(8,128)(2,1)} %param.13) | copy-start | bytes 393220

commit v5 on v4

--- a/solution.py
+++ b/solution.py
@@ -69,7 +69,7 @@
     pl.semaphore_wait(barrier, reach - 1)
 
     started = []
-    for off in range(0, reach):
+    for off in [0, *range(cols, reach), *range(1, cols)]:
         for (varies, spans), source, target, (sent, got, kept) in zip(
             plan, sources, targets, [sems[3 * n : 3 * n + 3] for n in range(count)]
         ):
@@ -129,8 +129,9 @@
         pltpu.make_async_copy(source.at[me if varies else mine], target.at[base], kept).wait()
         unfold(target, open_ref, base)
 
-        def arrive(off, carry, slots=slots, base=base, source=source, target=target,
+        def arrive(step, carry, slots=slots, base=base, source=source, target=target,
                    open_ref=open_ref, sent=sent, got=got):
+            off = lax.rem(step + cols - 2, slots - 1) + 1
             back = lax.rem(base - off + slots, slots)
             arriving = pltpu.make_async_remote_copy(
                 src_ref=source.at[0],
@@ -188,7 +189,8 @@
         )
     pl.semaphore_wait(barrier, slots - 1)
 
-    def send(off, carry):
+    def send(step, carry):
+        off = lax.rem(step + cols - 2, slots - 1) + 1
         fold(lax.rem(base + off, slots))
         push(off, base).start()
         return carry

time: 361 us -> 359 us (level)
  no operation moved by 1% of the time
where the time goes in v5:
time: 359 us
  Pallas kernels  319 us (89%)
  other arithmetic  24 us (7%)
  matrix products  14 us (4%)
    pallas_call x2, Pallas kernels, exchange(): pl.pallas_call(functools.partial(exchange_kernel, plan, sizes, opened is...  168 us
    pallas_call x2, Pallas kernels, fold_exchange(): pl.pallas_call(functools.partial(fold_kernel, spans, sizes), out_shape=ja...  136 us
    pallas_call x2, Pallas kernels, product(): pl.pallas_call(functools.partial(product_kernel, turned), out_shape=jax.S...  15.3 us
    reduce_sum x4, other arithmetic, layer_norm(): variance = jnp.mean(centred * centred, axis=reduce_axis, keepdims=True)  8.75 us

profile of v5, /device:TPU:11, one launch (start us, length us, event | category | flops | bytes accessed | tf_op | source)
XLA Modules:
  0.0 358.8 jit_solution(1946344272946846271)
XLA Ops:
  0.0 2.7 convert_reduce_fusion
  2.8 4.4 %multiply_reduce_fusion.3 = f32[96,96]{1,0:T(8,128)S(1)} fusion(bf16[96,96,128]{2,1,0:T(8,128)(2,1)} %param.11, f32[96,96]{1,0:T(8,128)S(1)} %broadcast_multiply_fusion), kind=kLoop, calls=%fused_computation.58 | loop fusion | flops 4709376 | bytes 2433024 | tf_op jit(solution)/shard_map/reduce_sum | solution.py:16
  7.1 0.1 rsqrt.36
  7.2 0.1 div.45
  7.4 4.9 %fusion.35 = bf16[9216,128]{1,0:T(8,128)(2,1)S(1)} fusion(bf16[96,96,128]{2,1,0:T(8,128)(2,1)S(1)} %copy-done.3, f32[128]{0:T(128)S(1)} %copy-done.11, f32[9216]{0:T(1024)S(1)} %rsqrt.36, f32[9216]{0:T(1024)S(1)} %div.45), kind=kLoop, calls=%fused_computation.52 | loop fusion | flops 5898240 | bytes 4792832 | tf_op jit(solution)/shard_map/convert_element_type | solution.py:23
  12.3 2.6 convolution_bitcast_fusion.1
  15.0 2.5 fusion.19
  17.5 112.0 %shard_map.109 = (bf16[8,16,96,96]{3,2,1,0:T(8,128)(2,1)S(1)}, bf16[16,16,96,96]{3,2,1,0:T(8,128)(2,1)S(1)}) custom-call(bf16[8,16,9216]{2,1,0:T(8,128)(2,1)S(1)} %bitcast.53, bf16[8,16,9216]{2,1,0:T(8,128)(2,1)S(1)} %bitcast.52), custom_call_target="tpu_custom_call" | custom-call | tf_op jit(solution)/shard_map/pallas_call | solution.py:249
  129.5 4.9 %shard_map.110 = bf16[2,4,16,96,96]{4,3,2,1,0:T(8,128)(2,1)S(1)} custom-call(bf16[2,4,16,96,96]{4,3,2,1,0:T(8,128)(2,1)S(1)} %bitcast.57, bf16[4,4,16,96,96]{4,3,2,1,0:T(8,128)(2,1)S(1)} %bitcast.56), custom_call_target="tpu_custom_call" | custom-call | flops 905969664 | bytes 7077888 | tf_op jit(solution)/shard_map/pallas_call | solution.py:301
  134.4 0.0 copy-start.12
  134.4 30.1 %shard_map.111 = bf16[8,16,9216]{2,1,0:T(8,128)(2,1)S(1)} custom-call(bf16[8,16,96,96]{3,2,1,0:T(8,128)(2,1)S(1)} %bitcast.51), custom_call_target="tpu_custom_call" | custom-call | tf_op jit(solution)/shard_map/pallas_call | solution.py:216
  164.5 0.0 copy-start.14
  164.5 0.4 convert_reduce_fusion.1
  164.9 0.7 multiply_reduce_fusion.2
  165.6 0.7 fusion.32
  166.4 1.4 fusion.9
  167.8 0.2 copy-done.4
  168.0 2.0 fusion.37
  170.1 2.7 multiply_reduce_fusion.1
  172.9 2.8 convolution_bitcast_fusion
  175.7 2.5 fusion.11
  178.3 55.8 %shard_map.112 = (bf16[8,16,96,96]{3,2,1,0:T(8,128)(2,1)S(1)}, bf16[8,16,96,96]{3,2,1,0:T(8,128)(2,1)S(1)}) custom-call(bf16[8,16,9216]{2,1,0:T(8,128)(2,1)S(1)} %bitcast.55, bf16[8,16,9216]{2,1,0:T(8,128)(2,1)S(1)} %bitcast.54), custom_call_target="tpu_custom_call" | custom-call | tf_op jit(solution)/shard_map/pallas_call | solution.py:249
  234.1 10.4 %shard_map.113 = bf16[4,4,16,96,96]{4,3,2,1,0:T(8,128)(2,1)S(1)} custom-call(bf16[2,4,16,96,96]{4,3,2,1,0:T(8,128)(2,1)S(1)} %bitcast.58, bf16[2,4,16,96,96]{4,3,2,1,0:T(8,128)(2,1)S(1)} %bitcast.59), custom_call_target="tpu_custom_call" | custom-call | flops 905969664 | bytes 4718592 | tf_op jit(solution)/shard_map/pallas_call | solution.py:301
  244.5 106.1 %shard_map.114 = bf16[16,16,9216]{2,1,0:T(8,128)(2,1)S(1)} custom-call(bf16[16,16,96,96]{3,2,1,0:T(8,128)(2,1)S(1)} %bitcast.50), custom_call_target="tpu_custom_call" | custom-call | tf_op jit(solution)/shard_map/pallas_call | solution.py:216
  350.6 0.7 fusion.36
  351.4 1.0 multiply_reduce_fusion
  352.4 0.7 fusion.29
  353.1 0.4 slice-done
  353.5 0.1 slice-done.1
  353.6 0.1 copy-done.15
  353.7 2.7 fusion.10
  356.4 2.4 fusion.7
  (39 shorter events, 0.2 us)
Async XLA Ops:
  0.0 12.3 %copy-start = (bf16[128,512]{1,0:T(8,128)(2,1)S(1)}, bf16[128,512]{1,0:T(8,128)(2,1)}, u32[]{:S(2)}) copy-start(bf16[128,512]{1,0:T(8,128)(2,1)} %param.13) | copy-start | bytes 393220
  0.0 7.3 %copy-start.3 = (bf16[96,96,128]{2,1,0:T(8,128)(2,1)S(1)}, bf16[96,96,128]{2,1,0:T(8,128)(2,1)}, u32[]{:S(2)}) copy-start(bf16[96,96,128]{2,1,0:T(8,128)(2,1)} %param.11) | copy-start | bytes 7077892
  0.0 7.3 %copy-start.11 = (f32[128]{0:T(128)S(1)}, f32[128]{0:T(128)}, u32[]{:S(2)}) copy-start(f32[128]{0:T(128)} %param.12) | copy-start | bytes 1540
  12.3 2.7 copy-start.5
  134.4 31.3 %copy-start.12 = (f32[128]{0:T(128)S(1)}, f32[128]{0:T(128)}, u32[]{:S(2)}) copy-start(f32[128]{0:T(128)} %param.15) | copy-start | bytes 1540
  164.5 1.9 copy-start.6
  164.5 1.9 copy-start.14
  166.4 1.7 copy-start.4
  166.4 1.7 copy-start.8
  170.1 5.7 %copy-start.2 = (f32[9216,128]{1,0:T(8,128)}, f32[9216,128]{1,0:T(8,128)S(1)}, u32[]{:S(2)}) copy-start(f32[9216,128]{1,0:T(8,128)S(1)} %get-tuple-element.20) | copy-start | bytes 14155780
  170.1 2.8 copy-start.7
  170.1 2.8 copy-start.10
  351.3 2.2 slice-start
  351.3 1.1 copy-start.13
  351.3 2.3 slice-start.1
  352.3 1.3 copy-start.15
  353.7 2.7 copy-start.9
  353.7 5.1 %copy-start.1 = (bf16[128,512]{1,0:T(8,128)(2,1)S(1)}, bf16[128,512]{1,0:T(8,128)(2,1)}, u32[]{:S(2)}) copy-start(bf16[128,512]{1,0:T(8,128)(2,1)} %param.13) | copy-start | bytes 393220
